TPU v7x, 256 devices: a whole 4x4x8 slice. The times are simulated.
256 devices in a mesh: lon: 32 (over x_lo, z, core), lat: 8 (over y, x_hi).
Axes of the slice: x: 4 (x_hi: 2, x_lo: 2; x = x_hi * 2 + x_lo), y: 4, z: 8, core: 2. Of those that a mesh axis runs over, the one named last changes fastest.
Arguments:
- thermal_anomaly_field: float32 [15, 768, 4096], P(None, 'lat', 'lon'), may hold values from -6 to 6
- saltiness_anomaly: float32 [15, 768, 4096], P(None, 'lat', 'lon'), may hold values from -6 to 6
- zonal_boundary_flow: float32 [15, 768, 4096], P(None, 'lat', 'lon'), may hold values from -3 to 3
- meridional_boundary_flow: float32 [15, 768, 4096], P(None, 'lat', 'lon'), may hold values from -3 to 3
- navigable_water_flag: int32 [15, 768, 4096], P(None, 'lat', 'lon'), may hold values 0 or 1
- flooded_layer_tally: int32 [768, 4096], P('lat', 'lon'), may hold values from 0 to 15, as said below
Outputs:
- temperature_next: float32 [15, 768, 4096], P(None, 'lat', 'lon')
- salinity_next: float32 [15, 768, 4096], P(None, 'lat', 'lon')
- zonal_next: float32 [15, 768, 4096], P(None, 'lat', 'lon')
- meridional_next: float32 [15, 768, 4096], P(None, 'lat', 'lon')
Inputs may be any that keep to these rules, and one draw needn't show every extreme that they name: `flooded_layer_tally`: land columns have 0.
All inputs are finite; a program needn't handle non-finite values. No bound on the sum of `navigable_water_flag` on one device may be relied on, other than what follows from the above.
Results may differ from a plain program's by a relative error of at most 0.0003.
Values sent between devices are 32-bit elements; how exact they have to be, the bound alone decides.
No kernel may reach another device: no remote copies, remote signals or barrier semaphores. Data moves between devices by JAX's collectives and lax.ppermute only.
A program may use at most 64 MiB of HBM per device.

v0:
```python
import jax
import jax.numpy as jnp
from jax import lax
from jax.experimental import pallas as pl
from jax.experimental.pallas import tpu as pltpu
from jax.sharding import PartitionSpec as P

TIME_STEP = 0.2
KAPPA = 0.1
VISCOSITY = 0.1
VERTICAL = 0.5
GRAVITY = 0.2
THERMAL = 0.3
HALINE = 0.2
CORIOLIS = 0.5

LEVELS = 15
ROWS = 96
COLS = 128
TILE = 8
BLOCKS = ROWS // TILE
PAD = TILE
TALL = ROWS + 2 * PAD
FIELDS = 5
STATE = 4
SIGNS = (1.0, 1.0, -1.0, -1.0, 1.0)
PACK = 16 * 2 * FIELDS
WET_AT = 8 * LEVELS
EDGE_AT = WET_AT + 32
MESSAGE = EDGE_AT + 16
VMEM = pltpu.CompilerParams(vmem_limit_bytes=48 * 1024 * 1024)
F32 = jnp.float32


def roll(x, shift, axis):
    return pltpu.roll(x, shift % x.shape[axis], axis)


def iota(shape, axis):
    return lax.broadcasted_iota(jnp.int32, shape, axis)


def links_of(wet):
    out = []
    above, ratio = None, None
    for k in range(LEVELS):
        below = VERTICAL * wet[k] * wet[k + 1] if k < LEVELS - 1 else None
        pivot = 1.0 + (below if below is not None else 0.0)
        if above is not None:
            pivot = pivot + above - above * ratio
        inverse = 1.0 / pivot
        ratio = below * inverse if below is not None else None
        out.append((above, inverse, ratio))
        above = below
    return out


def column_step(get, faces, links, spin):
    mix = KAPPA
    half = 0.5 * GRAVITY * TIME_STEP
    done = [[], [], [], []]
    forward = []
    east_sum = north_sum = None
    for k in range(LEVELS):
        w, oe, ow, on, os = faces(k)
        u, uE, uW, uN, uS = (get(2, k, 0, 0), get(2, k, 0, 1), get(2, k, 0, -1), get(2, k, 1, 0), get(2, k, -1, 0))
        v, vE, vW, vN, vS = (get(3, k, 0, 0), get(3, k, 0, 1), get(3, k, 0, -1), get(3, k, 1, 0), get(3, k, -1, 0))
        uNW, vSE = get(2, k, 1, -1), get(3, k, -1, 1)
        coef = []
        for speed, face in ((u, oe), (uW, ow), (v, on), (vS, os)):
            low = jnp.maximum(speed, 0.0) + mix
            coef.append((face * low, face * (low - speed)))
        tracers = []
        east, north = [], []
        for f in (0, 1):
            c, cE, cW, cN, cS = (get(f, k, 0, 0), get(f, k, 0, 1), get(f, k, 0, -1), get(f, k, 1, 0), get(f, k, -1, 0))
            out_e = coef[0][0] * c - coef[0][1] * cE
            out_w = coef[1][0] * cW - coef[1][1] * c
            out_n = coef[2][0] * c - coef[2][1] * cN
            out_s = coef[3][0] * cS - coef[3][1] * c
            tracers.append(w * (c - TIME_STEP * ((out_e - out_w) + (out_n - out_s))))
            east.append(cE - c)
            north.append(cN - c)
        up, inverse, _ = links(k)
        if k:
            before = forward[-1]
            forward.append(tuple((x + up * y) * inverse for x, y in zip(tracers, before)))
        else:
            forward.append(tuple(x * inverse for x in tracers))
        east_now = (half * HALINE) * east[1] - (half * THERMAL) * east[0]
        north_now = (half * HALINE) * north[1] - (half * THERMAL) * north[0]
        east_p = east_now if k == 0 else east_sum + east_now
        north_p = north_now if k == 0 else north_sum + north_now
        east_sum, north_sum = east_p + east_now, north_p + north_now
        turn = TIME_STEP * VISCOSITY
        done[2].append(oe * ((1.0 - 4.0 * turn) * u + spin * ((v + vS) + (vE + vSE)) - east_p
                             + turn * ((uE + uW) + (uN + uS))))
        done[3].append(on * ((1.0 - 4.0 * turn) * v - spin * ((u + uN) + (uW + uNW)) - north_p
                             + turn * ((vE + vW) + (vN + vS))))
    for f in (0, 1):
        value = forward[-1][f]
        back = [value]
        for k in range(LEVELS - 2, -1, -1):
            value = forward[k][f] + links(k)[2] * value
            back.append(value)
        done[f] = back[::-1]
    return done


def spin_of(row_index):
    angle = jnp.pi * ((row_index + 0.5) / (8.0 * ROWS) - 0.3)
    return (0.25 * TIME_STEP * CORIOLIS) * jnp.sin(angle)


def memo(shift, fields):
    held = {}

    def get(f, k, dj, di):
        key = (f, k, dj, di)
        if key not in held:
            held[key] = fields[f][k] if dj == 0 and di == 0 else shift(fields[f][k], dj, di)
        return held[key]

    return get


def faces_of(get):
    def faces(k):
        w = get(4, k, 0, 0)
        return (w, w * get(4, k, 0, 1), w * get(4, k, 0, -1), w * get(4, k, 1, 0), w * get(4, k, -1, 0))

    return faces


def pack_kernel(place, t, s, u, v, flag, tally, col_p, col_q, own_cols, rows, scratch):
    odd = place[1] % 2 == 1
    lane = iota((ROWS, COLS), 1)
    deep = tally[...]
    for f in range(FIELDS):
        gathered = jnp.zeros((ROWS, COLS), F32)
        for k in range(LEVELS):
            if f < STATE:
                x = (t, s, u, v)[f][k]
            else:
                x = jnp.where(k < deep, flag[k], 0).astype(F32)
            gathered = jnp.where((lane >= 8 * k) & (lane < 8 * k + 4), roll(x, 8 * k + 2, 1), gathered)
            at = 8 * k + 2 * f if f < STATE else WET_AT + 2 * k
            rows[0, at:at + 2, :] = x[0:2]
            rows[1, at:at + 2, :] = x[ROWS - 2:ROWS]
        scratch[0:ROWS, :] = gathered
        scratch[ROWS:COLS, :] = jnp.zeros((COLS - ROWS, COLS), F32)
        own_cols[f] = scratch[...].T
        for c in range(2):
            last = own_cols[f, pl.ds(c, 16, stride=8), :]
            first = own_cols[f, pl.ds(2 + c, 16, stride=8), :]
            at = (2 * f + c) * 16
            col_p[at:at + 16, :] = jnp.where(odd, first, last)
            col_q[at:at + 16, :] = jnp.where(odd, last, first)
    rows[0, WET_AT + 30:EDGE_AT, :] = jnp.zeros((2, COLS), F32)
    rows[1, WET_AT + 30:EDGE_AT, :] = jnp.zeros((2, COLS), F32)


def spread_kernel(place, got_p, got_q, own_cols, rows, strip, ghost, own, to_x, to_y, turned):
    odd = place[1] % 2 == 1
    lat_odd = place[0] % 2 == 1
    fold = place[0] == 7
    for f in range(FIELDS):
        for c in range(2):
            at = (2 * f + c) * 16
            a, b = got_p[at:at + 16, :], got_q[at:at + 16, :]
            west, east = jnp.where(odd, a, b), jnp.where(odd, b, a)
            strip[f, pl.ds(c, 16, stride=8), :] = west
            strip[f, pl.ds(4 + c, 16, stride=8), :] = east
            turned[pl.ds(c, 16, stride=8), :] = west
            turned[pl.ds(2 + c, 16, stride=8), :] = east
            turned[pl.ds(4 + c, 16, stride=8), :] = west
            turned[pl.ds(6 + c, 16, stride=8), :] = east
        strip[f, pl.ds(2, 16, stride=8), :] = own_cols[f, pl.ds(2, 16, stride=8), :]
        strip[f, pl.ds(3, 16, stride=8), :] = own_cols[f, pl.ds(1, 16, stride=8), :]
        strip[f, pl.ds(6, 16, stride=8), :] = jnp.zeros((16, COLS), F32)
        strip[f, pl.ds(7, 16, stride=8), :] = jnp.zeros((16, COLS), F32)
        ghost[f] = turned[...].T
        own[0, EDGE_AT + 2 * f:EDGE_AT + 2 * f + 2, :] = ghost[f, 0:2, :]
        own[1, EDGE_AT + 2 * f:EDGE_AT + 2 * f + 2, :] = ghost[f, ROWS - 2:ROWS, :]
    for side in range(2):
        own[side, 0:EDGE_AT, :] = rows[side]
        own[side, EDGE_AT + 2 * FIELDS:MESSAGE, :] = jnp.zeros((MESSAGE - EDGE_AT - 2 * FIELDS, COLS), F32)
    low, high = own[0], own[1]
    to_x[...] = jnp.where(lat_odd, high, low)
    to_y[...] = jnp.where(lat_odd, low, high)

    @pl.when(fold)
    def _():
        a, b = iota((COLS, COLS), 0), iota((COLS, COLS), 1)
        mirror = (a + b == COLS - 1).astype(F32)
        mirror_edge = ((a // 8 == b // 8) & (a % 8 < 4) & (a % 8 + b % 8 == 3)).astype(F32)
        to_x[0:EDGE_AT, :] = jnp.dot(own[1, 0:EDGE_AT, :], mirror, precision=lax.Precision.HIGHEST,
                                     preferred_element_type=F32)
        to_x[EDGE_AT:MESSAGE, :] = jnp.dot(own[1, EDGE_AT:MESSAGE, :], mirror_edge,
                                           precision=lax.Precision.HIGHEST, preferred_element_type=F32)


def inner_kernel(place, t, s, u, v, flag, tally, strip, ghost, t_out, s_out, u_out, v_out, inner, inner_ghost,
                 field, east, west, wet, oe, ow, on, link, ghost1, turned):
    first_row = place[0] * ROWS
    lane = iota((TILE, COLS), 1)
    sub = iota((TILE, COLS), 0)

    def at(b):
        return pl.multiple_of(b * TILE + PAD, TILE)

    def sides(x, edge, k):
        h = roll(edge, 126 - 8 * k, 1)
        return (roll(jnp.where(lane == 0, h, x), COLS - 1, 1), roll(jnp.where(lane == COLS - 1, h, x), 1, 1))

    def wet_block(b, carry):
        r = at(b)
        src = pl.ds(pl.multiple_of(b * TILE, TILE), TILE)
        deep = tally[src, :]
        edge = ghost[4, src, :]
        column = []
        for k in range(LEVELS):
            w = jnp.where(k < deep, flag[k, src, :], 0).astype(F32)
            column.append(w)
            wet[k, pl.ds(r, TILE), :] = w
            e, a = sides(w, edge, k)
            oe[k, pl.ds(r, TILE), :] = w * e
            ow[k, pl.ds(r, TILE), :] = w * a
        for k, (up, inverse, ratio) in enumerate(links_of(column)):
            if up is not None:
                link[0, k, src, :] = up
            link[1, k, src, :] = inverse
            if ratio is not None:
                link[2, k, src, :] = ratio
        return carry

    lax.fori_loop(0, BLOCKS, wet_block, 0)

    def north_block(b, carry):
        r = at(b)
        for k in range(LEVELS):
            on[k, pl.ds(r, TILE), :] = wet[k, pl.ds(r, TILE), :] * wet[k, pl.ds(r + 1, TILE), :]
        return carry

    lax.fori_loop(0, BLOCKS, north_block, 0)

    def strip_shift(x, dj, di):
        if di:
            x = roll(x, -di, 0)
        return roll(x, -dj, 1) if dj else x

    values = [[strip[f, 8 * k:8 * k + 8, :] for k in range(LEVELS)] for f in range(FIELDS)]
    get = memo(strip_shift, values)
    row = (first_row + iota((1, COLS), 1)).astype(F32)
    links = links_of(values[4])
    moved = column_step(get, faces_of(get), lambda k: links[k], spin_of(row))
    for f in range(STATE):
        for k in range(LEVELS):
            turned[8 * k:8 * k + 8, :] = jnp.where(sub == 1, moved[f][k], roll(moved[f][k], -2, 0))
        turned[8 * LEVELS:COLS, :] = jnp.zeros((COLS - 8 * LEVELS, COLS), F32)
        ghost1[f] = turned[...].T

    for step in range(2):
        def spread_block(b, carry, step=step):
            r = at(b)
            src = pl.ds(pl.multiple_of(b * TILE, TILE), TILE)
            for f in range(STATE):
                edge = (ghost, ghost1)[step][f, src, :]
                for k in range(LEVELS):
                    if step == 0:
                        x = (t, s, u, v)[f][k, src, :]
                        field[0, f, k, pl.ds(r, TILE), :] = x
                    else:
                        x = field[1, f, k, pl.ds(r, TILE), :]
                    e, a = sides(x, edge, k)
                    east[f, k, pl.ds(r, TILE), :] = e
                    west[f, k, pl.ds(r, TILE), :] = a
            return carry

        lax.fori_loop(0, BLOCKS, spread_block, 0)

        def step_block(b, carry, step=step):
            r = at(b)
            src = pl.ds(pl.multiple_of(b * TILE, TILE), TILE)

            def get(f, k, dj, di):
                ref = (field.at[step], east, west)[di]
                return ref[f, k, pl.ds(r + dj, TILE), :]

            def faces(k):
                here = pl.ds(r, TILE)
                return (wet[k, here, :], oe[k, here, :], ow[k, here, :], on[k, here, :], on[k, pl.ds(r - 1, TILE), :])

            def links(k):
                return tuple(link[i, k, src, :] for i in range(3))

            row = (first_row + b * TILE + iota((TILE, COLS), 0)).astype(F32)
            moved = column_step(get, faces, links, spin_of(row))
            for f in range(STATE):
                for k in range(LEVELS):
                    if step == 0:
                        field[1, f, k, pl.ds(r, TILE), :] = moved[f][k]
                    else:
                        (t_out, s_out, u_out, v_out)[f][k, src, :] = moved[f][k]
            return carry

        lax.fori_loop(0, BLOCKS, step_block, 0)

    for f in range(FIELDS):
        for k in range(LEVELS):
            src = field.at[1, f, k] if f < STATE else wet.at[k]
            inner[0, f, k] = src[PAD - 1:PAD + 7, :]
            inner[1, f, k] = src[PAD + 93:PAD + 101, :]
        edge = ghost1[f] if f < STATE else ghost[4]
        inner_ghost[0, f] = roll(edge[0:8], 1, 0)
        inner_ghost[1, f] = edge[93:101]


def edge_kernel(folds, place, own, got, inner, inner_ghost, t, s, u, v, t_out, s_out, u_out, v_out, lower, upper):
    lat = place[0]
    high = place[2] == 1
    fold = (lat == 7) & high if folds else None
    mine, theirs = own[0], got[...]
    if folds:
        theirs = jnp.where((lat == 0) & jnp.logical_not(high), 0.0, theirs)
    lower[...] = jnp.where(high, mine, theirs)
    upper[...] = jnp.where(high, theirs, mine)
    sub = iota((TILE, COLS), 0)
    lane = iota((TILE, COLS), 1)

    def stack(at, sign):
        a, b = lower[at:at + 2, :], upper[at:at + 2, :]
        if not folds:
            return jnp.concatenate([a, b, a, b], axis=0)
        second = jnp.where(fold, sign * b[1:2], b[0:1])
        return jnp.concatenate([a, second, b[1:2], b, sign * a[1:2], a[1:2]], axis=0)

    def spread(edge, k):
        return roll(edge, 126 - 8 * k, 1)

    values = []
    for f in range(FIELDS):
        edge = stack(EDGE_AT + 2 * f, SIGNS[f])
        levels = []
        for k in range(LEVELS):
            x = stack(8 * k + 2 * f if f < STATE else WET_AT + 2 * k, SIGNS[f])
            levels.append(jnp.concatenate([x, spread(edge, k)], axis=1))
        values.append(levels)

    back = iota((TILE, 2 * COLS), 0) >= jnp.where(fold, 4, TILE) if folds else None

    def ring_shift(x, dj, di):
        if dj:
            x = roll(x, -dj, 0)
        if di:
            there = roll(x, -di, 1)
            x = jnp.where(back, roll(x, di, 1), there) if folds else there
        return x

    def rows_of(start, shape):
        return (lat * ROWS + start + iota(shape, 0)).astype(F32)

    get = memo(ring_shift, values)
    links = links_of(values[4])
    start = jnp.where(high, ROWS - 2, -2)
    row = rows_of(start, (TILE, 1))
    if folds:
        row = jnp.where(fold, float(8 * ROWS - 1), row)
    moved = column_step(get, faces_of(get), lambda k: links[k], spin_of(row))

    def settle(x, f):
        ring = x
        up = roll(ring, 1, 0)
        down = roll(ring, -1, 0)
        if folds:
            up = jnp.where(sub == jnp.where(fold, 3, TILE), SIGNS[f] * roll(ring, -2, 0), up)
        return jnp.where(high, up, down)

    fresh_at = jnp.where(high, 2, 0)
    fresh = (sub >= fresh_at) & (sub < fresh_at + 2)
    middles, ghosts = [], []
    for f in range(FIELDS):
        mids, eds = [], []
        near = inner_ghost[0, f]
        for k in range(LEVELS):
            part = moved[f][k] if f < STATE else values[4][k]
            mids.append(jnp.where(fresh, settle(part[:, :COLS], f), inner[0, f, k]))
            eds.append(jnp.where(fresh, settle(part[:, COLS:], f), spread(near, k)))
        middles.append(mids)
        ghosts.append(eds)
    held = {}

    def get2(f, k, dj, di):
        key = (f, k, dj, di)
        if key not in held:
            x = middles[f][k]
            if di == 1:
                x = roll(jnp.where(lane == 0, ghosts[f][k], x), COLS - 1, 1)
            elif di == -1:
                x = roll(jnp.where(lane == COLS - 1, ghosts[f][k], x), 1, 1)
            held[key] = roll(x, -dj, 0) if dj else x
        return held[key]

    links2 = links_of(middles[4])
    row2 = rows_of(jnp.where(high, ROWS - 3, -1), (TILE, 1))
    last = column_step(get2, faces_of(get2), lambda k: links2[k], spin_of(row2))
    write_at = jnp.where(high, TILE - 2, 0)
    write = (sub >= write_at) & (sub < write_at + 2)
    for f in range(STATE):
        for k in range(LEVELS):
            x = jnp.where(high, roll(last[f][k], 5, 0), roll(last[f][k], -1, 0))
            (t_out, s_out, u_out, v_out)[f][k] = jnp.where(write, x, (t, s, u, v)[f][k])


def whole(shape):
    return pl.BlockSpec(shape, lambda *_: (0,) * len(shape))


def call(kernel, place, args, outs, scratch, cost):
    return pl.pallas_call(
        kernel,
        out_shape=[jax.ShapeDtypeStruct(o, F32) for o in outs],
        grid_spec=pltpu.PrefetchScalarGridSpec(
            num_scalar_prefetch=1,
            grid=(1,),
            in_specs=[whole(a.shape) for a in args],
            out_specs=[whole(o) for o in outs],
            scratch_shapes=[pltpu.VMEM(x, F32) for x in scratch],
        ),
        compiler_params=VMEM,
        cost_estimate=cost,
    )(place, *args)


def edge_call(folds, place, own, got, inner, inner_ghost, fields):
    def block(shape, index):
        return pl.BlockSpec(shape, index)

    strip = pl.BlockSpec((LEVELS, TILE, COLS), lambda i, p: (0, p[2] * (BLOCKS - 1), 0))
    return pl.pallas_call(
        lambda *refs: edge_kernel(folds, *refs),
        out_shape=[jax.ShapeDtypeStruct(x.shape, F32) for x in fields],
        grid_spec=pltpu.PrefetchScalarGridSpec(
            num_scalar_prefetch=1,
            grid=(1,),
            in_specs=[
                block((1, MESSAGE, COLS), lambda i, p: (p[2], 0, 0)),
                whole((MESSAGE, COLS)),
                block((1, FIELDS, LEVELS, TILE, COLS), lambda i, p: (p[2], 0, 0, 0, 0)),
                block((1, FIELDS, TILE, COLS), lambda i, p: (p[2], 0, 0, 0)),
            ] + [strip] * STATE,
            out_specs=[strip] * STATE,
            scratch_shapes=[pltpu.VMEM((MESSAGE, COLS), F32)] * 2,
        ),
        input_output_aliases={5 + f: f for f in range(STATE)},
        compiler_params=VMEM,
        cost_estimate=pl.CostEstimate(flops=2_000_000, bytes_accessed=2_000_000, transcendentals=0),
    )(place, own, got, inner, inner_ghost, *fields)


def device(lon, lat, lats, lons):
    return lon % lons * lats + lat


def body(t, s, u, v, flag, tally):
    lons, lats = lax.axis_size("lon"), lax.axis_size("lat")
    lat, lon = lax.axis_index("lat"), lax.axis_index("lon")
    side_x = lat % 2
    place = jnp.stack([lat, lon, side_x]).astype(jnp.int32)
    place_y = jnp.stack([lat, lon, 1 - side_x]).astype(jnp.int32)
    pairs_p, pairs_q, pairs_x, pairs_y = [], [], [], []
    for a in range(lats):
        for o in range(lons):
            here = device(o, a, lats, lons)
            pairs_p.append((here, device(o ^ 1, a, lats, lons)))
            pairs_q.append((here, device(o + 1 if o % 2 else o - 1, a, lats, lons)))
            pairs_y.append((here, device(o, a ^ 1, lats, lons)))
            next_lat = a + 1 if a % 2 else a - 1
            inside = 0 <= next_lat < lats
            pairs_x.append((here, device(o, next_lat, lats, lons) if inside else device(lons - 1 - o, a, lats, lons)))

    def send(x, pairs):
        return lax.ppermute(x, ("lon", "lat"), pairs)

    small = pl.CostEstimate(flops=1_000_000, bytes_accessed=4_000_000, transcendentals=0)
    large = pl.CostEstimate(flops=100_000_000, bytes_accessed=8_000_000, transcendentals=0)
    col_p, col_q, own_cols, rows = call(
        pack_kernel, place, (t, s, u, v, flag, tally),
        [(PACK, COLS), (PACK, COLS), (FIELDS, COLS, COLS), (2, EDGE_AT, COLS)],
        [(COLS, COLS)], small)
    got_p, got_q = send(col_p, pairs_p), send(col_q, pairs_q)
    strip, ghost, own, to_x, to_y = call(
        spread_kernel, place, (got_p, got_q, own_cols, rows),
        [(FIELDS, COLS, COLS), (FIELDS, COLS, COLS), (2, MESSAGE, COLS), (MESSAGE, COLS), (MESSAGE, COLS)],
        [(COLS, COLS)], small)
    got_x, got_y = send(to_x, pairs_x), send(to_y, pairs_y)
    tall = (LEVELS, TALL, COLS)
    *fields, inner, inner_ghost = call(
        inner_kernel, place, (t, s, u, v, flag, tally, strip, ghost),
        [(LEVELS, ROWS, COLS)] * STATE + [(2, FIELDS, LEVELS, TILE, COLS), (2, FIELDS, TILE, COLS)],
        [(2, STATE) + tall, (STATE,) + tall, (STATE,) + tall, tall, tall, tall, tall,
         (3, LEVELS, ROWS, COLS), (STATE, COLS, COLS), (COLS, COLS)], large)
    fields = edge_call(False, place_y, own, got_y, inner, inner_ghost, fields)
    fields = edge_call(True, place, own, got_x, inner, inner_ghost, fields)
    return tuple(fields)


def solution(mesh):
    cut = P(None, "lat", "lon")
    return jax.shard_map(
        body,
        mesh=mesh,
        in_specs=(cut, cut, cut, cut, cut, P("lat", "lon")),
        out_specs=(cut, cut, cut, cut),
        check_vma=False,
    )
```

profile of v0, /device:TPU:24, one launch (start us, length us, event | category | flops | bytes accessed | tf_op | source)
XLA Modules:
  0.0 79.7 jit_solution(16621669394092400549)
XLA Ops:
  0.6 0.1 pad_add_fusion.place.refs_0_
  0.7 0.0 copy-start
  0.7 1.1 %copy-done = f32[15,96,128]{2,1,0:T(8,128)S(1)} copy-done((f32[15,96,128]{2,1,0:T(8,128)S(1)}, f32[15,96,128]{2,1,0:T(8,128)}, u32[]{:S(2)}) %copy-start) | copy-done | bytes 737304
  1.8 0.0 copy-start.2
  1.8 1.1 %copy-done.2 = f32[15,96,128]{2,1,0:T(8,128)S(1)} copy-done((f32[15,96,128]{2,1,0:T(8,128)S(1)}, f32[15,96,128]{2,1,0:T(8,128)}, u32[]{:S(2)}) %copy-start.2) | copy-done | bytes 737304
  3.0 0.0 copy-start.4
  3.0 1.1 %copy-done.4 = f32[15,96,128]{2,1,0:T(8,128)S(1)} copy-done((f32[15,96,128]{2,1,0:T(8,128)S(1)}, f32[15,96,128]{2,1,0:T(8,128)}, u32[]{:S(2)}) %copy-start.4) | copy-done | bytes 737304
  4.1 0.0 copy-start.6
  4.1 1.1 %copy-done.6 = f32[15,96,128]{2,1,0:T(8,128)S(1)} copy-done((f32[15,96,128]{2,1,0:T(8,128)S(1)}, f32[15,96,128]{2,1,0:T(8,128)}, u32[]{:S(2)}) %copy-start.6) | copy-done | bytes 737304
  5.2 0.0 copy-start.8
  5.2 1.1 %copy-done.8 = s32[15,96,128]{2,1,0:T(8,128)S(1)} copy-done((s32[15,96,128]{2,1,0:T(8,128)S(1)}, s32[15,96,128]{2,1,0:T(8,128)}, u32[]{:S(2)}) %copy-start.8) | copy-done | bytes 737304
  6.3 0.0 copy-start.10
  6.3 0.8 copy-done.10
  7.1 0.0 copy-start.1
  7.1 0.0 copy-start.3
  7.1 0.0 copy-start.5
  7.1 0.0 copy-start.7
  7.1 2.5 %shard_map.93 = (f32[160,128]{1,0:T(8,128)}, f32[160,128]{1,0:T(8,128)}, f32[5,128,128]{2,1,0:T(8,128)S(1)}, f32[2,152,128]{2,1,0:T(8,128)S(1)}) custom-call(s32[3]{0:T(128)S(1)} %pad_add_fusion.place.refs_0_, f32[15,96,128]{2,1,0:T(8,128)S(1)} %copy-done, f32[15,96,128]{2,1,0:T(8,128)S(1)} %copy-done.2, f32[15,96,128]{2,1,0:T(8,128)S(1)} %copy-done.4, ...), custom_call_target="tpu_custom_call" | custom-call | flops 1000000 | bytes 4000000 | tf_op jit(solution)/shard_map/pallas_call | solution.py:420
  9.6 0.0 collective-permute-start
  9.6 6.9 %collective-permute-start.1 = (f32[160,128]{1,0:T(8,128)}, f32[160,128]{1,0:T(8,128)}, u32[]{:S(2)}, u32[]{:S(2)}) collective-permute-start(f32[160,128]{1,0:T(8,128)} %get-tuple-element.24), channel_id=1, source_target_pairs={{0,248},{8,16},{16,8},{24,32},{32,24},{40,48},{48,40},{56,64},{64,... | collective-permute-start | bytes 245768 | tf_op jit(solution)/shard_map/ppermute | solution.py:483
  16.5 0.0 collective-permute-done.got_p
  16.5 2.4 %collective-permute-done.1.got_q = f32[160,128]{1,0:T(8,128)} collective-permute-done((f32[160,128]{1,0:T(8,128)}, f32[160,128]{1,0:T(8,128)}, u32[]{:S(2)}, u32[]{:S(2)}) %collective-permute-start.1) | collective-permute-done | bytes 81952 | tf_op jit(solution)/shard_map/ppermute | solution.py:483
  19.0 0.0 copy-start.11
  19.0 1.7 %shard_map.94 = (f32[5,128,128]{2,1,0:T(8,128)S(1)}, f32[5,128,128]{2,1,0:T(8,128)S(1)}, f32[2,168,128]{2,1,0:T(8,128)S(1)}, f32[168,128]{1,0:T(8,128)S(1)}, f32[168,128]{1,0:T(8,128)S(1)}) custom-call(s32[3]{0:T(128)S(1)} %pad_add_fusion.place.refs_0_, f32[160,128]{1,0:T(8,128)S(1)} %collective-permute-done.got_p, f32[160,128]{1,0:T(8,128)} %collective-permute-done.1.got_q, ...), custom_call_target="tpu_custom_call" | custom-call | flops 1000000 | bytes 4000000 | tf_op jit(solution)/shard_map/pallas_call | solution.py:420
  20.6 3.0 %collective-permute-start.2 = (f32[168,128]{1,0:T(8,128)S(1)}, f32[168,128]{1,0:T(8,128)S(1)}, u32[]{:S(2)}, u32[]{:S(2)}) collective-permute-start(f32[168,128]{1,0:T(8,128)S(1)} %get-tuple-element.28), channel_id=1, source_target_pairs={{0,248},{8,240},{16,232},{24,224},{32,216},{40,208},{48,200},{56,1... | collective-permute-start | bytes 258056 | tf_op jit(solution)/shard_map/ppermute | solution.py:483
  23.6 4.0 %collective-permute-start.3 = (f32[168,128]{1,0:T(8,128)S(1)}, f32[168,128]{1,0:T(8,128)S(1)}, u32[]{:S(2)}, u32[]{:S(2)}) collective-permute-start(f32[168,128]{1,0:T(8,128)S(1)} %get-tuple-element.33), channel_id=1, source_target_pairs={{0,1},{8,9},{16,17},{24,25},{32,33},{40,41},{48,49},{56,57},{64,65... | collective-permute-start | bytes 258056 | tf_op jit(solution)/shard_map/ppermute | solution.py:483
  27.7 0.1 pad_add_fusion.2.refs_0_
  27.7 0.0 copy-done.1
  27.7 0.0 copy-done.3
  27.7 0.0 copy-done.5
  27.7 0.0 copy-done.7
  27.7 0.0 copy-done.11
  27.8 0.0 copy-start.9
  27.8 1.1 %copy-done.9 = s32[15,96,128]{2,1,0:T(8,128)S(1)} copy-done((s32[15,96,128]{2,1,0:T(8,128)S(1)}, s32[15,96,128]{2,1,0:T(8,128)}, u32[]{:S(2)}) %copy-start.9) | copy-done | bytes 737304
  28.9 44.0 %shard_map.95 = (f32[15,96,128]{2,1,0:T(8,128)}, f32[15,96,128]{2,1,0:T(8,128)}, f32[15,96,128]{2,1,0:T(8,128)}, f32[15,96,128]{2,1,0:T(8,128)}, f32[2,5,15,8,12...) custom-call(s32[3]{0:T(128)S(1)} %pad_add_fusion.place.refs_0_, f32[15,96,128]{2,1,0:T(8,128)S(1)} %copy-done.1, ...), custom_call_target="tpu_custom_call" | custom-call | flops 100000000 | bytes 8000000 | tf_op jit(solution)/shard_map/pallas_call | solution.py:420
  72.9 0.0 collective-permute-done.3.refs_2_
  72.9 3.3 %shard_map.96 = (f32[15,96,128]{2,1,0:T(8,128)}, f32[15,96,128]{2,1,0:T(8,128)}, f32[15,96,128]{2,1,0:T(8,128)}, f32[15,96,128]{2,1,0:T(8,128)}) custom-call(s32[3]{0:T(128)S(1)} %pad_add_fusion.2.refs_0_, f32[2,168,128]{2,1,0:T(8,128)S(1)} %get-tuple-element.27.refs_1_, ...), custom_call_target="tpu_custom_call", output_to_operand_aliasing={{0}: (5, {}), {1}: (6, {}), {2}: (7, {}), {3}: (8, {})} | custom-call | flops 2000000 | bytes 2000000 | tf_op jit(solution)/shard_map/pallas_call | solution.py:440
  76.2 0.0 collective-permute-done.2.refs_2_
  76.2 3.5 %shard_map.97 = (f32[15,96,128]{2,1,0:T(8,128)}, f32[15,96,128]{2,1,0:T(8,128)}, f32[15,96,128]{2,1,0:T(8,128)}, f32[15,96,128]{2,1,0:T(8,128)}) custom-call(s32[3]{0:T(128)S(1)} %pad_add_fusion.place.refs_0_, f32[2,168,128]{2,1,0:T(8,128)S(1)} %get-tuple-element.27.refs_1_, ...), custom_call_target="tpu_custom_call", output_to_operand_aliasing={{0}: (5, {}), {1}: (6, {}), {2}: (7, {}), {3}: (8, {})} | custom-call | flops 2000000 | bytes 2000000 | tf_op jit(solution)/shard_map/pallas_call | solution.py:440
Async XLA Ops:
  0.7 1.1 %copy-start = (f32[15,96,128]{2,1,0:T(8,128)S(1)}, f32[15,96,128]{2,1,0:T(8,128)}, u32[]{:S(2)}) copy-start(f32[15,96,128]{2,1,0:T(8,128)} %t.3) | copy-start | bytes 2211844
  1.8 1.1 %copy-start.2 = (f32[15,96,128]{2,1,0:T(8,128)S(1)}, f32[15,96,128]{2,1,0:T(8,128)}, u32[]{:S(2)}) copy-start(f32[15,96,128]{2,1,0:T(8,128)} %s.3) | copy-start | bytes 2211844
  3.0 1.1 %copy-start.4 = (f32[15,96,128]{2,1,0:T(8,128)S(1)}, f32[15,96,128]{2,1,0:T(8,128)}, u32[]{:S(2)}) copy-start(f32[15,96,128]{2,1,0:T(8,128)} %u.3) | copy-start | bytes 2211844
  4.1 1.1 %copy-start.6 = (f32[15,96,128]{2,1,0:T(8,128)S(1)}, f32[15,96,128]{2,1,0:T(8,128)}, u32[]{:S(2)}) copy-start(f32[15,96,128]{2,1,0:T(8,128)} %v.3) | copy-start | bytes 2211844
  5.2 1.1 %copy-start.8 = (s32[15,96,128]{2,1,0:T(8,128)S(1)}, s32[15,96,128]{2,1,0:T(8,128)}, u32[]{:S(2)}) copy-start(s32[15,96,128]{2,1,0:T(8,128)} %flag.3) | copy-start | bytes 2211844
  6.3 0.8 %copy-start.10 = (s32[96,128]{1,0:T(8,128)S(1)}, s32[96,128]{1,0:T(8,128)}, u32[]{:S(2)}) copy-start(s32[96,128]{1,0:T(8,128)} %tally.3) | copy-start | bytes 147460
  7.1 20.6 %copy-start.1 = (f32[15,96,128]{2,1,0:T(8,128)S(1)}, f32[15,96,128]{2,1,0:T(8,128)}, u32[]{:S(2)}) copy-start(f32[15,96,128]{2,1,0:T(8,128)} %t.3) | copy-start | bytes 2211844
  7.1 20.6 %copy-start.3 = (f32[15,96,128]{2,1,0:T(8,128)S(1)}, f32[15,96,128]{2,1,0:T(8,128)}, u32[]{:S(2)}) copy-start(f32[15,96,128]{2,1,0:T(8,128)} %s.3) | copy-start | bytes 2211844
  7.1 20.6 %copy-start.5 = (f32[15,96,128]{2,1,0:T(8,128)S(1)}, f32[15,96,128]{2,1,0:T(8,128)}, u32[]{:S(2)}) copy-start(f32[15,96,128]{2,1,0:T(8,128)} %u.3) | copy-start | bytes 2211844
  7.1 20.6 %copy-start.7 = (f32[15,96,128]{2,1,0:T(8,128)S(1)}, f32[15,96,128]{2,1,0:T(8,128)}, u32[]{:S(2)}) copy-start(f32[15,96,128]{2,1,0:T(8,128)} %v.3) | copy-start | bytes 2211844
  9.6 6.9 %collective-permute-start = (f32[160,128]{1,0:T(8,128)}, f32[160,128]{1,0:T(8,128)S(1)}, u32[]{:S(2)}, u32[]{:S(2)}) collective-permute-start(f32[160,128]{1,0:T(8,128)} %get-tuple-element.23), channel_id=1, source_target_pairs={{0,8},{8,0},{16,24},{24,16},{32,40},{40,32},{48,56},{56,48},{64,72... | collective-permute-start | bytes 245768 | tf_op jit(solution)/shard_map/ppermute | solution.py:483
  9.6 9.3 %collective-permute-start.1 = (f32[160,128]{1,0:T(8,128)}, f32[160,128]{1,0:T(8,128)}, u32[]{:S(2)}, u32[]{:S(2)}) collective-permute-start(f32[160,128]{1,0:T(8,128)} %get-tuple-element.24), channel_id=1, source_target_pairs={{0,248},{8,16},{16,8},{24,32},{32,24},{40,48},{48,40},{56,64},{64,... | collective-permute-start | bytes 245768 | tf_op jit(solution)/shard_map/ppermute | solution.py:483
  19.0 8.8 %copy-start.11 = (s32[96,128]{1,0:T(8,128)S(1)}, s32[96,128]{1,0:T(8,128)}, u32[]{:S(2)}) copy-start(s32[96,128]{1,0:T(8,128)} %tally.3) | copy-start | bytes 147460
  20.6 55.6 %collective-permute-start.2 = (f32[168,128]{1,0:T(8,128)S(1)}, f32[168,128]{1,0:T(8,128)S(1)}, u32[]{:S(2)}, u32[]{:S(2)}) collective-permute-start(f32[168,128]{1,0:T(8,128)S(1)} %get-tuple-element.28), channel_id=1, source_target_pairs={{0,248},{8,240},{16,232},{24,224},{32,216},{40,208},{48,200},{56,1... | collective-permute-start | bytes 258056 | tf_op jit(solution)/shard_map/ppermute | solution.py:483
  23.6 49.2 %collective-permute-start.3 = (f32[168,128]{1,0:T(8,128)S(1)}, f32[168,128]{1,0:T(8,128)S(1)}, u32[]{:S(2)}, u32[]{:S(2)}) collective-permute-start(f32[168,128]{1,0:T(8,128)S(1)} %get-tuple-element.33), channel_id=1, source_target_pairs={{0,1},{8,9},{16,17},{24,25},{32,33},{40,41},{48,49},{56,57},{64,65... | collective-permute-start | bytes 258056 | tf_op jit(solution)/shard_map/ppermute | solution.py:483
  27.8 1.1 %copy-start.9 = (s32[15,96,128]{2,1,0:T(8,128)S(1)}, s32[15,96,128]{2,1,0:T(8,128)}, u32[]{:S(2)}) copy-start(s32[15,96,128]{2,1,0:T(8,128)} %flag.3) | copy-start | bytes 2211844
where the time goes:
time: 80.2 us; the launch traced here: 79.7 us
  Pallas kernels  55 us (69%)
  starting transfers between devices  13.9 us (17%)
  local copies, waits for them, and re-layouts  7.51 us (9%)
  waiting for transfers between devices  2.44 us (3%)
    pallas_call x3, Pallas kernels, call(): pl.pallas_call(kernel, out_shape=[jax.ShapeDtypeStruct(o, F32) for o in o...  48.2 us
    ppermute x4, starting transfers between devices, send(): return lax.ppermute(x, ('lon', 'lat'), pairs)  13.9 us
    unnamed x24, local copies, waits for them, and re-layouts  7.51 us
    pallas_call x2, Pallas kernels, edge_call(): pl.pallas_call(lambda *refs: edge_kernel(folds, *refs), out_shape=[jax.Sh...  6.81 us
    ppermute x4, waiting for transfers between devices, send(): return lax.ppermute(x, ('lon', 'lat'), pairs)  2.44 us
  transfers between devices with their start and end apart: 4, of which 1 were waited for; matrix products, arithmetic and copies ran while one was open for 0% of the time, Pallas kernels for 59%

commit v1 on v0

v1 whole, which is shorter than its diff:
```python
import jax
import jax.numpy as jnp
from jax import lax
from jax.experimental import pallas as pl
from jax.experimental.pallas import tpu as pltpu
from jax.sharding import PartitionSpec as P

TIME_STEP = 0.2
KAPPA = 0.1
VISCOSITY = 0.1
VERTICAL = 0.5
GRAVITY = 0.2
THERMAL = 0.3
HALINE = 0.2
CORIOLIS = 0.5

LEVELS = 15
ROWS = 96
COLS = 128
TILE = 8
BLOCKS = ROWS // TILE
PAD = TILE
TALL = ROWS + 2 * PAD
FIELDS = 5
STATE = 4
SIGNS = (1.0, 1.0, -1.0, -1.0, 1.0)
PACK = 16 * 2 * FIELDS
WET_AT = 8 * LEVELS
EDGE_AT = WET_AT + 32
MESSAGE = EDGE_AT + 16
F32 = jnp.float32


def roll(x, shift, axis):
    return pltpu.roll(x, shift % x.shape[axis], axis)


def iota(shape, axis):
    return lax.broadcasted_iota(jnp.int32, shape, axis)


def links_of(wet):
    out = []
    above, ratio = None, None
    for k in range(LEVELS):
        below = VERTICAL * wet[k] * wet[k + 1] if k < LEVELS - 1 else None
        pivot = 1.0 + (below if below is not None else 0.0)
        if above is not None:
            pivot = pivot + above - above * ratio
        inverse = 1.0 / pivot
        ratio = below * inverse if below is not None else None
        out.append((above, inverse, ratio))
        above = below
    return out


def column_step(get, faces, links, spin, west=None, south=None):
    mix = KAPPA
    half = 0.5 * GRAVITY * TIME_STEP
    done = [[], [], [], []]
    forward, loose = [], []
    east_sum = north_sum = None
    for k in range(LEVELS):
        w, oe, ow, on, os = faces(k)
        u, uE, uW, uN, uS = (get(2, k, 0, 0), get(2, k, 0, 1), get(2, k, 0, -1), get(2, k, 1, 0), get(2, k, -1, 0))
        v, vE, vW, vN, vS = (get(3, k, 0, 0), get(3, k, 0, 1), get(3, k, 0, -1), get(3, k, 1, 0), get(3, k, -1, 0))
        uNW, vSE = get(2, k, 1, -1), get(3, k, -1, 1)
        coef = []
        for speed, face in ((u, oe), (uW, ow), (v, on), (vS, os)):
            if face is None:
                coef.append(None)
                continue
            low = jnp.maximum(speed, 0.0) + mix
            coef.append((face * low, face * (low - speed)))
        tracers = []
        east, north = [], []
        for f in (0, 1):
            c, cE, cN = get(f, k, 0, 0), get(f, k, 0, 1), get(f, k, 1, 0)
            out_e = coef[0][0] * c - coef[0][1] * cE
            if west is None:
                out_e = out_e - (coef[1][0] * get(f, k, 0, -1) - coef[1][1] * c)
            out_n = coef[2][0] * c - coef[2][1] * cN
            out_s = south(f, k, out_n) if south else coef[3][0] * get(f, k, -1, 0) - coef[3][1] * c
            tracers.append((c - TIME_STEP * (out_n - out_s), out_e))
            east.append(cE - c)
            north.append(cN - c)
        loose.append(tracers)
        east_now = (half * HALINE) * east[1] - (half * THERMAL) * east[0]
        north_now = (half * HALINE) * north[1] - (half * THERMAL) * north[0]
        east_p = east_now if k == 0 else east_sum + east_now
        north_p = north_now if k == 0 else north_sum + north_now
        east_sum, north_sum = east_p + east_now, north_p + north_now
        turn = TIME_STEP * VISCOSITY
        done[2].append(oe * ((1.0 - 4.0 * turn) * u + spin * ((v + vS) + (vE + vSE)) - east_p
                             + turn * ((uE + uW) + (uN + uS))))
        done[3].append(on * ((1.0 - 4.0 * turn) * v - spin * ((u + uN) + (uW + uNW)) - north_p
                             + turn * ((vE + vW) + (vN + vS))))
    for k in range(LEVELS):
        w = faces(k)[0]
        up, inverse, _ = links(k)
        now = []
        for f in (0, 1):
            kept, out = loose[k][f]
            x = w * (kept - TIME_STEP * (out - west(f, k, out) if west else out))
            now.append((x + up * forward[-1][f]) * inverse if k else x * inverse)
        forward.append(now)
    for f in (0, 1):
        value = forward[-1][f]
        back = [value]
        for k in range(LEVELS - 2, -1, -1):
            value = forward[k][f] + links(k)[2] * value
            back.append(value)
        done[f] = back[::-1]
    return done


def spin_of(row_index):
    angle = jnp.pi * ((row_index + 0.5) / (8.0 * ROWS) - 0.3)
    return (0.25 * TIME_STEP * CORIOLIS) * jnp.sin(angle)


SHIFTS = {0: (), 1: (), 2: (1, -1), 3: (-1, 1), 4: ()}


def eager(shift, fields):
    held = {}
    count = len(fields)
    for f in range(count):
        for k in range(LEVELS):
            held[f, k, 0, 0] = fields[f][k]
    for dj, di in ((0, 1), (0, -1), (1, 0), (-1, 0)):
        for f in range(count):
            for k in range(LEVELS):
                held[f, k, dj, di] = shift(fields[f][k], dj, di)
    for f in (2, 3):
        dj, di = SHIFTS[f]
        for k in range(LEVELS):
            held[f, k, dj, di] = shift(held[f, k, 0, di], dj, 0)
    return lambda f, k, dj, di: held[f, k, dj, di]


def faces_of(get):
    def faces(k):
        w = get(4, k, 0, 0)
        return (w, w * get(4, k, 0, 1), w * get(4, k, 0, -1), w * get(4, k, 1, 0), w * get(4, k, -1, 0))

    return faces


def split3(x):
    a = x.astype(jnp.bfloat16)
    rest = x - a.astype(F32)
    b = rest.astype(jnp.bfloat16)
    return a, b, (rest - b.astype(F32)).astype(jnp.bfloat16)


def picker(k, moves):
    source, target = iota((COLS, COLS), 0) - 8 * k, iota((COLS, COLS), 1)
    hit = jnp.zeros((COLS, COLS), jnp.bool_)
    for lane, p in moves.items():
        hit = hit | ((target == lane) & (source == p))
    return hit.astype(jnp.bfloat16)


def picked(terms, pick):
    return sum(jnp.dot(x, pick, preferred_element_type=F32) for x in terms)


AROUND = {126: 0, 127: 1, 0: 2, 1: 3}
NEXT1 = {127: 1, 0: 6}
OWN1 = {0: 2, 127: 5}
FLUX1 = {0: 1}
FACE = {0: 1, 127: 2}


def pack_kernel(place, t, s, u, v, flag, tally, col_p, col_q, own_cols, rows, wet, field, held_flag, held_tally, sems,
                gathered):
    odd = place[1] % 2 == 1
    lane = iota((TILE, COLS), 1)
    sub = iota((TILE, COLS), 0)
    group = jnp.where(lane % 8 < 4, lane // 8, -1)
    inside = pl.ds(PAD, ROWS)
    copies = [pltpu.make_async_copy(x, field.at[f, :, inside, :], sems.at[f]) for f, x in enumerate((t, s, u, v))]
    copies.append(pltpu.make_async_copy(flag, held_flag, sems.at[4]))
    copies.append(pltpu.make_async_copy(tally, held_tally, sems.at[5]))
    for f in (4, 5, 0, 1, 2, 3):
        copies[f].start()
    for f in (4, 0, 1, 2, 3):
        copies[f].wait()
        if f == STATE:
            copies[5].wait()
        for b in range(BLOCKS):
            at = PAD + TILE * b
            out = jnp.zeros((TILE, COLS), F32)
            for k in range(LEVELS):
                if f < STATE:
                    x = field[f, k, at:at + TILE, :]
                else:
                    here = slice(TILE * b, TILE * b + TILE)
                    x = jnp.where(k < held_tally[here, :], held_flag[k, here, :], 0).astype(F32)
                    wet[k, at:at + TILE, :] = x
                out = jnp.where(group == k, roll(x, 8 * k + 2, 1), out)
            gathered[f, TILE * b:TILE * b + TILE, :] = out
        gathered[f, ROWS:COLS, :] = jnp.zeros((COLS - ROWS, COLS), F32)
    for f in range(FIELDS):
        own_cols[f] = gathered[f].T
    for side, first in ((0, PAD), (1, PAD + ROWS - 2)):
        for m in range(LEVELS + 4):
            parts = []
            for i in range(4):
                at = first - 2 * i
                if m < LEVELS:
                    parts.append(field[i, m, at:at + TILE, :])
                else:
                    k = min(4 * (m - LEVELS) + i, LEVELS - 1)
                    parts.append(wet[k, at:at + TILE, :])
            rows[side, TILE * m:TILE * m + TILE, :] = jnp.where(
                sub < 2, parts[0], jnp.where(sub < 4, parts[1], jnp.where(sub < 6, parts[2], parts[3])))
    for f in range(FIELDS):
        for c in range(2):
            last = own_cols[f, pl.ds(c, 16, stride=8), :]
            first = own_cols[f, pl.ds(2 + c, 16, stride=8), :]
            at = (2 * f + c) * 16
            col_p[at:at + 16, :] = jnp.where(odd, first, last)
            col_q[at:at + 16, :] = jnp.where(odd, last, first)


def spread_kernel(place, got_p, got_q, own_cols, rows, strip, ghost, own, to_x, to_y, turned):
    odd = place[1] % 2 == 1
    lat_odd = place[0] % 2 == 1
    fold = place[0] == 7
    for f in range(FIELDS):
        for c in range(2):
            at = (2 * f + c) * 16
            a, b = got_p[at:at + 16, :], got_q[at:at + 16, :]
            west, east = jnp.where(odd, a, b), jnp.where(odd, b, a)
            strip[f, pl.ds(c, 16, stride=8), :] = west
            strip[f, pl.ds(6 + c, 16, stride=8), :] = east
            strip[f, pl.ds(2 + c, 16, stride=8), :] = own_cols[f, pl.ds(2 + c, 16, stride=8), :]
            strip[f, pl.ds(4 + c, 16, stride=8), :] = own_cols[f, pl.ds(c, 16, stride=8), :]
            turned[f, pl.ds(c, 16, stride=8), :] = west
            turned[f, pl.ds(2 + c, 16, stride=8), :] = east
            turned[f, pl.ds(4 + c, 16, stride=8), :] = west
            turned[f, pl.ds(6 + c, 16, stride=8), :] = east
    for f in range(FIELDS):
        ghost[f] = turned[f].T
    for f in range(FIELDS):
        own[0, EDGE_AT + 2 * f:EDGE_AT + 2 * f + 2, :] = ghost[f, 0:2, :]
        own[1, EDGE_AT + 2 * f:EDGE_AT + 2 * f + 2, :] = ghost[f, ROWS - 2:ROWS, :]
    for side in range(2):
        own[side, 0:EDGE_AT, :] = rows[side]
        own[side, EDGE_AT + 2 * FIELDS:MESSAGE, :] = jnp.zeros((MESSAGE - EDGE_AT - 2 * FIELDS, COLS), F32)
    low, high = own[0], own[1]
    to_x[...] = jnp.where(lat_odd, high, low)
    to_y[...] = jnp.where(lat_odd, low, high)

    @pl.when(fold)
    def _():
        a, b = iota((COLS, COLS), 0), iota((COLS, COLS), 1)
        mirror = (a + b == COLS - 1).astype(jnp.bfloat16)
        mirror_edge = ((a // 8 == b // 8) & (a % 8 < 4) & (a % 8 + b % 8 == 3)).astype(jnp.bfloat16)
        to_x[0:EDGE_AT, :] = picked(split3(own[1, 0:EDGE_AT, :]), mirror)
        to_x[EDGE_AT:MESSAGE, :] = picked(split3(own[1, EDGE_AT:MESSAGE, :]), mirror_edge)


def rows_at(b):
    return pl.multiple_of(b * TILE + PAD, TILE)


def first_kernel(place, t, s, u, v, wet, field1, open_e, link, spin, field, flux, sems):
    first_row = place[0] * ROWS
    copies = [pltpu.make_async_copy(x, field.at[f, :, pl.ds(PAD, ROWS), :], sems.at[f])
              for f, x in enumerate((t, s, u, v))]
    for c in copies:
        c.start()

    def face_block(b, carry):
        here = pl.ds(rows_at(b), TILE)
        src = pl.ds(pl.multiple_of(b * TILE, TILE), TILE)
        column = [wet[k, here, :] for k in range(LEVELS)]
        for k, w in enumerate(column):
            open_e[k, src, :] = w * roll(w, COLS - 1, 1)
        for k, (up, inverse, ratio) in enumerate(links_of(column)):
            if up is not None:
                link[0, k, src, :] = up
            link[1, k, src, :] = inverse
            if ratio is not None:
                link[2, k, src, :] = ratio
        row = (first_row + b * TILE + iota((TILE, COLS), 0)).astype(F32)
        spin[src, :] = spin_of(row)
        return carry

    lax.fori_loop(0, BLOCKS, face_block, 0)
    for c in copies:
        c.wait()

    def step_block(b, carry):
        r = rows_at(b)
        src = pl.ds(pl.multiple_of(b * TILE, TILE), TILE)

        def get(f, k, dj, di):
            x = field[f, k, pl.ds(r + dj, TILE), :]
            return roll(x, -di, 1) if di else x

        def faces(k):
            w = wet[k, pl.ds(r, TILE), :]
            return (w, open_e[k, src, :], None, w * wet[k, pl.ds(r + 1, TILE), :], None)

        def south(f, k, x):
            flux[f, k, pl.ds(r, TILE), :] = x
            return flux[f, k, pl.ds(r - 1, TILE), :]

        moved = column_step(get, faces, lambda k: tuple(link[i, k, src, :] for i in range(3)), spin[src, :],
                            lambda f, k, x: roll(x, 1, 1), south)
        for f in range(STATE):
            for k in range(LEVELS):
                field1[f, k, pl.ds(r, TILE), :] = moved[f][k]
        return carry

    lax.fori_loop(0, BLOCKS, step_block, 0)


def second_kernel(place, field1, wet, open_e, link, spin, strip, ghost, t, s, u, v, inner, inner_ghost,
                  state, outs, ghost1, turned, beside, face, flux, sems):
    first_row = place[0] * ROWS
    lane = iota((TILE, COLS), 1)

    def strip_shift(x, dj, di):
        if di:
            x = roll(x, -di, 0)
        return roll(x, -dj, 1) if dj else x

    values = [[strip[f, 8 * k:8 * k + 8, :] for k in range(LEVELS)] for f in range(FIELDS)]
    get1 = eager(strip_shift, values)
    row = (first_row + iota((1, COLS), 1)).astype(F32)
    links1 = links_of(values[4])
    moved = column_step(get1, faces_of(get1), lambda k: links1[k], spin_of(row))
    for f in range(STATE):
        for k in range(LEVELS):
            turned[f, 8 * k:8 * k + 8, :] = moved[f][k]
    faces1 = faces_of(get1)
    for f in range(2):
        for k in range(LEVELS):
            c, speed, face_e = moved[f][k], moved[2][k], faces1(k)[1]
            low = jnp.maximum(speed, 0.0) + KAPPA
            turned[STATE + f, 8 * k:8 * k + 8, :] = face_e * (low * c - (low - speed) * roll(c, -1, 0))
    for f in range(STATE + 2):
        turned[f, 8 * LEVELS:COLS, :] = jnp.zeros((COLS - 8 * LEVELS, COLS), F32)
    for f in range(STATE + 2):
        ghost1[f] = turned[f].T

    inside = pl.ds(PAD, ROWS)
    wide = iota((ROWS, COLS), 1)
    edge_lane = (wide == 0) | (wide == COLS - 1)
    face_terms = split3(ghost[4, 0:ROWS, :])
    terms = [split3(ghost1[f, 0:ROWS, :]) for f in range(STATE + 2)]
    for k in range(LEVELS):
        face[k] = picked(face_terms[:1], picker(k, FACE))
        around, own, into = picker(k, NEXT1), picker(k, OWN1), picker(k, FLUX1)
        for f in range(STATE):
            beside[f, k, inside, :] = picked(terms[f], around)
            if f < 2:
                beside[STATE + f, k, inside, :] = picked(terms[STATE + f], into)
            state[f, k, inside, :] = jnp.where(edge_lane, picked(terms[f], own), field1[f, k, inside, :])

    def copies(b):
        src = pl.ds(pl.multiple_of(b * TILE, TILE), TILE)
        return [pltpu.make_async_copy(outs.at[f, :, src, :], x.at[:, src, :], sems.at[f, b])
                for f, x in enumerate((t, s, u, v))]

    def step_block(b, carry):
        r = rows_at(b)
        src = pl.ds(pl.multiple_of(b * TILE, TILE), TILE)

        def get(f, k, dj, di):
            here = pl.ds(r + dj, TILE)
            x = state[f, k, here, :]
            if di == 0:
                return x
            return roll(jnp.where(lane == (0 if di > 0 else COLS - 1), beside[f, k, here, :], x), -di, 1)

        def faces(k):
            w = wet[k, pl.ds(r, TILE), :]
            across = w * face[k, src, :]
            return (w, jnp.where(lane == COLS - 1, across, open_e[k, src, :]), None,
                    w * wet[k, pl.ds(r + 1, TILE), :], None)

        def west(f, k, x):
            return jnp.where(lane == 0, beside[STATE + f, k, pl.ds(r, TILE), :], roll(x, 1, 1))

        def south(f, k, x):
            flux[f, k, pl.ds(r, TILE), :] = x
            return flux[f, k, pl.ds(r - 1, TILE), :]

        moved = column_step(get, faces, lambda k: tuple(link[i, k, src, :] for i in range(3)), spin[src, :], west, south)
        for f in range(STATE):
            for k in range(LEVELS):
                outs[f, k, src, :] = moved[f][k]
        for c in copies(b):
            c.start()
        return carry

    lax.fori_loop(0, BLOCKS, step_block, 0)

    for f in range(FIELDS):
        for k in range(LEVELS):
            src = state.at[f, k] if f < STATE else wet.at[k]
            inner[0, f, k] = src[PAD - 1:PAD + 7, :]
            inner[1, f, k] = src[PAD + 93:PAD + 101, :]
        edge = ghost1[f] if f < STATE else ghost[4]
        inner_ghost[0, f] = roll(edge[0:8], 1, 0)
        inner_ghost[1, f] = edge[93:101]

    def drain(b, carry):
        for c in copies(b):
            c.wait()
        return carry

    lax.fori_loop(0, BLOCKS, drain, 0)


def edge_kernel(folds, place, own, got, inner, inner_ghost, t, s, u, v, t_out, s_out, u_out, v_out, lower, upper):
    lat = place[0]
    high = place[2] == 1
    fold = (lat == 7) & high if folds else None
    mine, theirs = own[0], got[...]
    if folds:
        theirs = jnp.where((lat == 0) & jnp.logical_not(high), 0.0, theirs)
    lower[...] = jnp.where(high, mine, theirs)
    upper[...] = jnp.where(high, theirs, mine)
    sub = iota((TILE, COLS), 0)
    lane = iota((TILE, COLS), 1)

    def stack(at, sign):
        a, b = lower[at:at + 2, :], upper[at:at + 2, :]
        if not folds:
            return jnp.concatenate([a, b, a, b], axis=0)
        second = jnp.where(fold, sign * b[1:2], b[0:1])
        return jnp.concatenate([a, second, b[1:2], b, sign * a[1:2], a[1:2]], axis=0)

    edges = [stack(EDGE_AT + 2 * f, SIGNS[f]) for f in range(FIELDS)]
    edge_terms = split3(jnp.concatenate(edges, axis=0))
    near_terms = split3(jnp.concatenate([inner_ghost[0, f] for f in range(STATE)], axis=0))
    near_wet = split3(inner_ghost[0, STATE])[:1]
    spreads, nears = [[] for _ in range(FIELDS)], [[] for _ in range(FIELDS)]
    for k in range(LEVELS):
        around = picker(k, AROUND)
        found = picked(edge_terms, around)
        near = picked(near_terms, picker(k, NEXT1))
        for f in range(FIELDS):
            spreads[f].append(found[TILE * f:TILE * f + TILE])
        for f in range(STATE):
            nears[f].append(near[TILE * f:TILE * f + TILE])
        nears[STATE].append(picked(near_wet, around))
    values = [[jnp.concatenate([stack(8 * k + 2 * f if f < STATE else WET_AT + 2 * k, SIGNS[f]), spreads[f][k]], axis=1)
               for k in range(LEVELS)] for f in range(FIELDS)]

    back = iota((TILE, 2 * COLS), 0) >= jnp.where(fold, 4, TILE) if folds else None

    def ring_shift(x, dj, di):
        if dj:
            x = roll(x, -dj, 0)
        if di:
            there = roll(x, -di, 1)
            x = jnp.where(back, roll(x, di, 1), there) if folds else there
        return x

    def rows_of(start, shape):
        return (lat * ROWS + start + iota(shape, 0)).astype(F32)

    get = eager(ring_shift, values)
    links = links_of(values[4])
    start = jnp.where(high, ROWS - 2, -2)
    row = rows_of(start, (TILE, 1))
    if folds:
        row = jnp.where(fold, float(8 * ROWS - 1), row)
    moved = column_step(get, faces_of(get), lambda k: links[k], spin_of(row))

    def settle(x, f):
        ring = x
        up = roll(ring, 1, 0)
        down = roll(ring, -1, 0)
        if folds:
            up = jnp.where(sub == jnp.where(fold, 3, TILE), SIGNS[f] * roll(ring, -2, 0), up)
        return jnp.where(high, up, down)

    fresh_at = jnp.where(high, 2, 0)
    fresh = (sub >= fresh_at) & (sub < fresh_at + 2)
    middles, ghosts = [], []
    for f in range(FIELDS):
        mids, eds = [], []
        for k in range(LEVELS):
            part = moved[f][k] if f < STATE else values[4][k]
            mids.append(jnp.where(fresh, settle(part[:, :COLS], f), inner[0, f, k]))
            eds.append(jnp.where(fresh, settle(part[:, COLS:], f), nears[f][k]))
        middles.append(mids)
        ghosts.append(eds)
    for f in range(FIELDS):
        middles[f] = list(zip(middles[f], ghosts[f]))

    def shift2(pair, dj, di):
        x, ghosted = pair
        if di == 1:
            return roll(jnp.where(lane == 0, ghosted, x), COLS - 1, 1), None
        if di == -1:
            return roll(jnp.where(lane == COLS - 1, ghosted, x), 1, 1), None
        return roll(x, -dj, 0), None

    pairs = eager(shift2, middles)

    def get2(f, k, dj, di):
        return pairs(f, k, dj, di)[0]

    links2 = links_of([x for x, _ in middles[4]])
    row2 = rows_of(jnp.where(high, ROWS - 3, -1), (TILE, 1))
    last = column_step(get2, faces_of(get2), lambda k: links2[k], spin_of(row2))
    write_at = jnp.where(high, TILE - 2, 0)
    write = (sub >= write_at) & (sub < write_at + 2)
    for f in range(STATE):
        for k in range(LEVELS):
            x = jnp.where(high, roll(last[f][k], 5, 0), roll(last[f][k], -1, 0))
            (t_out, s_out, u_out, v_out)[f][k] = jnp.where(write, x, (t, s, u, v)[f][k])


def limit(mebibytes):
    return pltpu.CompilerParams(vmem_limit_bytes=mebibytes * 1024 * 1024)


def whole(shape):
    return pl.BlockSpec(shape, lambda *_: (0,) * len(shape))


def call(kernel, place, args, outs, scratch, mebibytes, flops, far_in=0, far_out=0):
    vmem, hbm = pl.BlockSpec(memory_space=pltpu.VMEM), pl.BlockSpec(memory_space=pltpu.HBM)
    args = [pltpu.with_memory_space_constraint(a, pltpu.HBM if i < far_in else pltpu.VMEM) for i, a in enumerate(args)]
    return pl.pallas_call(
        kernel,
        out_shape=[jax.ShapeDtypeStruct(o, F32) if i < far_out else pltpu.VMEM(o, F32) for i, o in enumerate(outs)],
        in_specs=[pl.BlockSpec(memory_space=pltpu.SMEM)] + [hbm if i < far_in else vmem for i in range(len(args))],
        out_specs=[hbm if i < far_out else vmem for i in range(len(outs))],
        scratch_shapes=[pltpu.VMEM(x, F32) if isinstance(x, tuple) else x for x in scratch],
        compiler_params=limit(mebibytes),
        cost_estimate=pl.CostEstimate(flops=flops, bytes_accessed=4_000_000, transcendentals=0),
    )(place, *args)


def edge_call(folds, place, own, got, inner, inner_ghost, fields):
    def block(shape, index):
        return pl.BlockSpec(shape, index)

    strip = pl.BlockSpec((LEVELS, TILE, COLS), lambda i, p: (0, p[2] * (BLOCKS - 1), 0))
    return pl.pallas_call(
        lambda *refs: edge_kernel(folds, *refs),
        out_shape=[jax.ShapeDtypeStruct(x.shape, F32) for x in fields],
        grid_spec=pltpu.PrefetchScalarGridSpec(
            num_scalar_prefetch=1,
            grid=(1,),
            in_specs=[
                block((1, MESSAGE, COLS), lambda i, p: (p[2], 0, 0)),
                whole((MESSAGE, COLS)),
                block((1, FIELDS, LEVELS, TILE, COLS), lambda i, p: (p[2], 0, 0, 0, 0)),
                block((1, FIELDS, TILE, COLS), lambda i, p: (p[2], 0, 0, 0)),
            ] + [strip] * STATE,
            out_specs=[strip] * STATE,
            scratch_shapes=[pltpu.VMEM((MESSAGE, COLS), F32)] * 2,
        ),
        input_output_aliases={5 + f: f for f in range(STATE)},
        compiler_params=limit(16),
        cost_estimate=pl.CostEstimate(flops=2_000_000, bytes_accessed=2_000_000, transcendentals=0),
    )(place, own, got, inner, inner_ghost, *fields)


def device(lon, lat, lats, lons):
    return lon % lons * lats + lat


def body(t, s, u, v, flag, tally):
    lons, lats = lax.axis_size("lon"), lax.axis_size("lat")
    lat, lon = lax.axis_index("lat"), lax.axis_index("lon")
    side_x = lat % 2
    place = jnp.stack([lat, lon, side_x]).astype(jnp.int32)
    place_y = jnp.stack([lat, lon, 1 - side_x]).astype(jnp.int32)
    pairs_p, pairs_q, pairs_x, pairs_y = [], [], [], []
    for a in range(lats):
        for o in range(lons):
            here = device(o, a, lats, lons)
            pairs_p.append((here, device(o ^ 1, a, lats, lons)))
            pairs_q.append((here, device(o + 1 if o % 2 else o - 1, a, lats, lons)))
            pairs_y.append((here, device(o, a ^ 1, lats, lons)))
            next_lat = a + 1 if a % 2 else a - 1
            inside = 0 <= next_lat < lats
            pairs_x.append((here, device(o, next_lat, lats, lons) if inside else device(lons - 1 - o, a, lats, lons)))

    def send(x, pairs):
        return lax.ppermute(x, ("lon", "lat"), pairs)

    deep, tall, square = (LEVELS, ROWS, COLS), (LEVELS, TALL, COLS), (FIELDS, COLS, COLS)
    message = (MESSAGE, COLS)
    col_p, col_q, own_cols, rows, wet = call(
        pack_kernel, place, (t, s, u, v, flag, tally), [(PACK, COLS), (PACK, COLS), square, (2, EDGE_AT, COLS), tall],
        [(STATE,) + tall, pltpu.VMEM(deep, jnp.int32), pltpu.VMEM((ROWS, COLS), jnp.int32), pltpu.SemaphoreType.DMA((6,)), square],
        12, 1_000_000, far_in=6)
    got_p, got_q = send(col_p, pairs_p), send(col_q, pairs_q)
    field1, open_e, link, spin = call(
        first_kernel, place, (t, s, u, v, wet), [(STATE,) + tall, deep, (3,) + deep, (ROWS, COLS)],
        [(STATE,) + tall, (2,) + tall, pltpu.SemaphoreType.DMA((STATE,))], 12, 40_000_000, far_in=STATE)
    strip, ghost, own, to_x, to_y = call(
        spread_kernel, place, (got_p, got_q, own_cols, rows), [square, square, (2, MESSAGE, COLS), message, message],
        [square], 4, 1_000_000)
    got_x, got_y = send(to_x, pairs_x), send(to_y, pairs_y)
    *fields, inner, inner_ghost = call(
        second_kernel, place, (field1, wet, open_e, link, spin, strip, ghost),
        [deep] * STATE + [(2, FIELDS, LEVELS, TILE, COLS), (2, FIELDS, TILE, COLS)],
        [(STATE,) + tall, (STATE,) + deep, (STATE + 2, COLS, COLS), (STATE + 2, COLS, COLS), (STATE + 2,) + tall, deep,
         (2,) + tall,
         pltpu.SemaphoreType.DMA((STATE, BLOCKS))], 20, 50_000_000, far_out=STATE)
    fields = edge_call(False, place_y, own, got_y, inner, inner_ghost, fields)
    fields = edge_call(True, place, own, got_x, inner, inner_ghost, fields)
    return tuple(fields)


def solution(mesh):
    cut = P(None, "lat", "lon")
    return jax.shard_map(
        body,
        mesh=mesh,
        in_specs=(cut, cut, cut, cut, cut, P("lat", "lon")),
        out_specs=(cut, cut, cut, cut),
        check_vma=False,
    )
```

time: 80.2 us -> 38.9 us (0.49)
  the two profiles are of different devices: /device:TPU:24 before, /device:TPU:8 now
where the time goes in v1:
time: 38.9 us; the launch traced here: 38.6 us
  Pallas kernels  26.2 us (67%)
  starting transfers between devices  11.6 us (30%)
  between operations  0.7 us (2%)
    pallas_call x4, Pallas kernels, call(): pl.pallas_call(kernel, out_shape=[jax.ShapeDtypeStruct(o, F32) if i < far...  19.2 us
    ppermute x4, starting transfers between devices, send(): return lax.ppermute(x, ('lon', 'lat'), pairs)  11.6 us
    pallas_call x2, Pallas kernels, edge_call(): pl.pallas_call(lambda *refs: edge_kernel(folds, *refs), out_shape=[jax.Sh...  6.96 us
  transfers between devices with their start and end apart: 4, of which 0 were waited for; matrix products, arithmetic and copies ran while one was open for 0% of the time, Pallas kernels for 48%

profile of v1, /device:TPU:8, one launch (start us, length us, event | category | flops | bytes accessed | tf_op | source)
XLA Modules:
  0.0 38.6 jit_solution(11829856102135661056)
XLA Ops:
  0.6 0.1 pad_add_fusion.place.refs_0_
  0.7 3.2 %shard_map.93 = (f32[160,128]{1,0:T(8,128)S(1)}, f32[160,128]{1,0:T(8,128)S(1)}, f32[5,128,128]{2,1,0:T(8,128)S(1)}, f32[2,152,128]{2,1,0:T(8,128)S(1)}, f32[15,112,128]{2,1,0:T(8,128)S(1)}) custom-call(s32[3]{0:T(128)S(1)} %pad_add_fusion.place.refs_0_, f32[15,96,128]{2,1,0:T(8,128)} %t.3, f32[15,96,128]{2,1,0:T(8,128)} %s.3, f32[15,96,128]{2,1,0:T(8,128)} %u.3, ...), custom_call_target="tpu_custom_call" | custom-call | flops 1000000 | bytes 4000000 | tf_op jit(solution)/shard_map/pallas_call | solution.py:536
  3.9 0.1 collective-permute-start
  4.0 6.9 %collective-permute-start.1 = (f32[160,128]{1,0:T(8,128)S(1)}, f32[160,128]{1,0:T(8,128)S(1)}, u32[]{:S(2)}, u32[]{:S(2)}) collective-permute-start(f32[160,128]{1,0:T(8,128)S(1)} %get-tuple-element.29), channel_id=1, source_target_pairs={{0,248},{8,16},{16,8},{24,32},{32,24},{40,48},{48,40},{56,64},{64,... | collective-permute-start | bytes 245768 | tf_op jit(solution)/shard_map/ppermute | solution.py:595
  10.9 5.9 %shard_map.95 = (f32[4,15,112,128]{3,2,1,0:T(8,128)S(1)}, f32[15,96,128]{2,1,0:T(8,128)S(1)}, f32[3,15,96,128]{3,2,1,0:T(8,128)S(1)}, f32[96,128]{1,0:T(8,128)S(1)}) custom-call(s32[3]{0:T(128)S(1)} %pad_add_fusion.place.refs_0_, f32[15,96,128]{2,1,0:T(8,128)} %t.3, f32[15,96,128]{2,1,0:T(8,128)} %s.3, f32[15,96,128]{2,1,0:T(8,128)} %u.3, f32[15,96,128]{2,1,0:T(8,128)} %v.3, ...), custom_call_target="tpu_custom_call" | custom-call | flops 40000000 | bytes 4000000 | tf_op jit(solution)/shard_map/pallas_call | solution.py:536
  16.8 0.0 collective-permute-done.got_p
  16.8 0.0 collective-permute-done.1.got_q
  16.8 0.8 %shard_map.94 = (f32[5,128,128]{2,1,0:T(8,128)S(1)}, f32[5,128,128]{2,1,0:T(8,128)S(1)}, f32[2,168,128]{2,1,0:T(8,128)S(1)}, f32[168,128]{1,0:T(8,128)S(1)}, f32[168,128]{1,0:T(8,128)S(1)}) custom-call(s32[3]{0:T(128)S(1)} %pad_add_fusion.place.refs_0_, f32[160,128]{1,0:T(8,128)S(1)} %collective-permute-done.got_p, ...), custom_call_target="tpu_custom_call" | custom-call | flops 1000000 | bytes 4000000 | tf_op jit(solution)/shard_map/pallas_call | solution.py:536
  17.6 2.7 %collective-permute-start.2 = (f32[168,128]{1,0:T(8,128)S(1)}, f32[168,128]{1,0:T(8,128)S(1)}, u32[]{:S(2)}, u32[]{:S(2)}) collective-permute-start(f32[168,128]{1,0:T(8,128)S(1)} %get-tuple-element.33), channel_id=1, source_target_pairs={{0,248},{8,240},{16,232},{24,224},{32,216},{40,208},{48,200},{56,1... | collective-permute-start | bytes 258056 | tf_op jit(solution)/shard_map/ppermute | solution.py:595
  20.3 1.9 %collective-permute-start.3 = (f32[168,128]{1,0:T(8,128)S(1)}, f32[168,128]{1,0:T(8,128)S(1)}, u32[]{:S(2)}, u32[]{:S(2)}) collective-permute-start(f32[168,128]{1,0:T(8,128)S(1)} %get-tuple-element.43), channel_id=1, source_target_pairs={{0,1},{8,9},{16,17},{24,25},{32,33},{40,41},{48,49},{56,57},{64,65... | collective-permute-start | bytes 258056 | tf_op jit(solution)/shard_map/ppermute | solution.py:595
  22.2 0.1 pad_add_fusion.2.refs_0_
  22.3 9.3 %shard_map.96 = (f32[15,96,128]{2,1,0:T(8,128)}, f32[15,96,128]{2,1,0:T(8,128)}, f32[15,96,128]{2,1,0:T(8,128)}, f32[15,96,128]{2,1,0:T(8,128)}, f32[2,5,15,8,12...) custom-call(s32[3]{0:T(128)S(1)} %pad_add_fusion.place.refs_0_, f32[4,15,112,128]{3,2,1,0:T(8,128)S(1)} %get-tuple-element.35.field1, ...), custom_call_target="tpu_custom_call" | custom-call | flops 50000000 | bytes 4000000 | tf_op jit(solution)/shard_map/pallas_call | solution.py:536
  31.6 0.0 collective-permute-done.3.refs_2_
  31.7 3.4 %shard_map.97 = (f32[15,96,128]{2,1,0:T(8,128)}, f32[15,96,128]{2,1,0:T(8,128)}, f32[15,96,128]{2,1,0:T(8,128)}, f32[15,96,128]{2,1,0:T(8,128)}) custom-call(s32[3]{0:T(128)S(1)} %pad_add_fusion.2.refs_0_, f32[2,168,128]{2,1,0:T(8,128)S(1)} %get-tuple-element.32.refs_1_, ...), custom_call_target="tpu_custom_call", output_to_operand_aliasing={{0}: (5, {}), {1}: (6, {}), {2}: (7, {}), {3}: (8, {})} | custom-call | flops 2000000 | bytes 2000000 | tf_op jit(solution)/shard_map/pallas_call | solution.py:552
  35.1 0.0 collective-permute-done.2.refs_2_
  35.1 3.5 %shard_map.98 = (f32[15,96,128]{2,1,0:T(8,128)}, f32[15,96,128]{2,1,0:T(8,128)}, f32[15,96,128]{2,1,0:T(8,128)}, f32[15,96,128]{2,1,0:T(8,128)}) custom-call(s32[3]{0:T(128)S(1)} %pad_add_fusion.place.refs_0_, f32[2,168,128]{2,1,0:T(8,128)S(1)} %get-tuple-element.32.refs_1_, ...), custom_call_target="tpu_custom_call", output_to_operand_aliasing={{0}: (5, {}), {1}: (6, {}), {2}: (7, {}), {3}: (8, {})} | custom-call | flops 2000000 | bytes 2000000 | tf_op jit(solution)/shard_map/pallas_call | solution.py:552
Async XLA Ops:
  3.9 12.9 %collective-permute-start = (f32[160,128]{1,0:T(8,128)S(1)}, f32[160,128]{1,0:T(8,128)S(1)}, u32[]{:S(2)}, u32[]{:S(2)}) collective-permute-start(f32[160,128]{1,0:T(8,128)S(1)} %get-tuple-element.28), channel_id=1, source_target_pairs={{0,8},{8,0},{16,24},{24,16},{32,40},{40,32},{48,56},{56,48},{64,72... | collective-permute-start | bytes 245768 | tf_op jit(solution)/shard_map/ppermute | solution.py:595
  4.0 12.8 %collective-permute-start.1 = (f32[160,128]{1,0:T(8,128)S(1)}, f32[160,128]{1,0:T(8,128)S(1)}, u32[]{:S(2)}, u32[]{:S(2)}) collective-permute-start(f32[160,128]{1,0:T(8,128)S(1)} %get-tuple-element.29), channel_id=1, source_target_pairs={{0,248},{8,16},{16,8},{24,32},{32,24},{40,48},{48,40},{56,64},{64,... | collective-permute-start | bytes 245768 | tf_op jit(solution)/shard_map/ppermute | solution.py:595
  17.6 17.5 %collective-permute-start.2 = (f32[168,128]{1,0:T(8,128)S(1)}, f32[168,128]{1,0:T(8,128)S(1)}, u32[]{:S(2)}, u32[]{:S(2)}) collective-permute-start(f32[168,128]{1,0:T(8,128)S(1)} %get-tuple-element.33), channel_id=1, source_target_pairs={{0,248},{8,240},{16,232},{24,224},{32,216},{40,208},{48,200},{56,1... | collective-permute-start | bytes 258056 | tf_op jit(solution)/shard_map/ppermute | solution.py:595
  20.3 11.4 %collective-permute-start.3 = (f32[168,128]{1,0:T(8,128)S(1)}, f32[168,128]{1,0:T(8,128)S(1)}, u32[]{:S(2)}, u32[]{:S(2)}) collective-permute-start(f32[168,128]{1,0:T(8,128)S(1)} %get-tuple-element.43), channel_id=1, source_target_pairs={{0,1},{8,9},{16,17},{24,25},{32,33},{40,41},{48,49},{56,57},{64,65... | collective-permute-start | bytes 258056 | tf_op jit(solution)/shard_map/ppermute | solution.py:595

commit v2 on v1

v2 whole, which is shorter than its diff:
```python
import jax
import jax.numpy as jnp
from jax import lax
from jax.experimental import pallas as pl
from jax.experimental.pallas import tpu as pltpu
from jax.sharding import PartitionSpec as P

TIME_STEP = 0.2
KAPPA = 0.1
VISCOSITY = 0.1
VERTICAL = 0.5
GRAVITY = 0.2
THERMAL = 0.3
HALINE = 0.2
CORIOLIS = 0.5

LEVELS = 15
ROWS = 96
COLS = 128
TILE = 8
BLOCKS = ROWS // TILE
PAD = TILE
TALL = ROWS + 2 * PAD
FIELDS = 5
STATE = 4
GROUPS = STATE + 3
SIGNS = (1.0, 1.0, -1.0, -1.0, 1.0)
PACK = 16 * 2 * FIELDS
WET_AT = 8 * LEVELS
EDGE_AT = WET_AT + 32
MESSAGE = EDGE_AT + 16
F32 = jnp.float32


def roll(x, shift, axis):
    return pltpu.roll(x, shift % x.shape[axis], axis)


def iota(shape, axis):
    return lax.broadcasted_iota(jnp.int32, shape, axis)


def links_of(wet):
    out = []
    above, ratio = None, None
    for k in range(LEVELS):
        below = VERTICAL * wet[k] * wet[k + 1] if k < LEVELS - 1 else None
        pivot = 1.0 + (below if below is not None else 0.0)
        if above is not None:
            pivot = pivot + above - above * ratio
        inverse = 1.0 / pivot
        ratio = below * inverse if below is not None else None
        out.append((above, inverse, ratio))
        above = below
    return out


def column_step(get, faces, links, spin, west=None, south=None):
    mix = KAPPA
    half = 0.5 * GRAVITY * TIME_STEP
    done = [[], [], [], []]
    forward, loose = [], []
    east_sum = north_sum = None
    for k in range(LEVELS):
        w, oe, ow, on, os = faces(k)
        u, uE, uW, uN, uS = (get(2, k, 0, 0), get(2, k, 0, 1), get(2, k, 0, -1), get(2, k, 1, 0), get(2, k, -1, 0))
        v, vE, vW, vN, vS = (get(3, k, 0, 0), get(3, k, 0, 1), get(3, k, 0, -1), get(3, k, 1, 0), get(3, k, -1, 0))
        uNW, vSE = get(2, k, 1, -1), get(3, k, -1, 1)
        coef = []
        for speed, face in ((u, oe), (uW, ow), (v, on), (vS, os)):
            if face is None:
                coef.append(None)
                continue
            low = jnp.maximum(speed, 0.0) + mix
            coef.append((face * low, face * (low - speed)))
        tracers = []
        east, north = [], []
        for f in (0, 1):
            c, cE, cN = get(f, k, 0, 0), get(f, k, 0, 1), get(f, k, 1, 0)
            out_e = coef[0][0] * c - coef[0][1] * cE
            if west is None:
                out_e = out_e - (coef[1][0] * get(f, k, 0, -1) - coef[1][1] * c)
            out_n = coef[2][0] * c - coef[2][1] * cN
            out_s = south(f, k, out_n) if south else coef[3][0] * get(f, k, -1, 0) - coef[3][1] * c
            tracers.append((c - TIME_STEP * (out_n - out_s), out_e))
            east.append(cE - c)
            north.append(cN - c)
        loose.append(tracers)
        east_now = (half * HALINE) * east[1] - (half * THERMAL) * east[0]
        north_now = (half * HALINE) * north[1] - (half * THERMAL) * north[0]
        east_p = east_now if k == 0 else east_sum + east_now
        north_p = north_now if k == 0 else north_sum + north_now
        east_sum, north_sum = east_p + east_now, north_p + north_now
        turn = TIME_STEP * VISCOSITY
        done[2].append(oe * ((1.0 - 4.0 * turn) * u + spin * ((v + vS) + (vE + vSE)) - east_p
                             + turn * ((uE + uW) + (uN + uS))))
        done[3].append(on * ((1.0 - 4.0 * turn) * v - spin * ((u + uN) + (uW + uNW)) - north_p
                             + turn * ((vE + vW) + (vN + vS))))
    for k in range(LEVELS):
        w = faces(k)[0]
        up, inverse, _ = links(k)
        now = []
        for f in (0, 1):
            kept, out = loose[k][f]
            x = w * (kept - TIME_STEP * (out - west(f, k, out) if west else out))
            now.append((x + up * forward[-1][f]) * inverse if k else x * inverse)
        forward.append(now)
    for f in (0, 1):
        value = forward[-1][f]
        back = [value]
        for k in range(LEVELS - 2, -1, -1):
            value = forward[k][f] + links(k)[2] * value
            back.append(value)
        done[f] = back[::-1]
    return done


def spin_of(row_index):
    angle = jnp.pi * ((row_index + 0.5) / (8.0 * ROWS) - 0.3)
    return (0.25 * TIME_STEP * CORIOLIS) * jnp.sin(angle)


SHIFTS = {0: (), 1: (), 2: (1, -1), 3: (-1, 1), 4: ()}


def eager(shift, fields):
    held = {}
    count = len(fields)
    for f in range(count):
        for k in range(LEVELS):
            held[f, k, 0, 0] = fields[f][k]
    for dj, di in ((0, 1), (0, -1), (1, 0), (-1, 0)):
        for f in range(count):
            for k in range(LEVELS):
                held[f, k, dj, di] = shift(fields[f][k], dj, di)
    for f in (2, 3):
        dj, di = SHIFTS[f]
        for k in range(LEVELS):
            held[f, k, dj, di] = shift(held[f, k, 0, di], dj, 0)
    return lambda f, k, dj, di: held[f, k, dj, di]


def faces_of(get):
    def faces(k):
        w = get(4, k, 0, 0)
        return (w, w * get(4, k, 0, 1), w * get(4, k, 0, -1), w * get(4, k, 1, 0), w * get(4, k, -1, 0))

    return faces


def split3(x):
    a = x.astype(jnp.bfloat16)
    rest = x - a.astype(F32)
    b = rest.astype(jnp.bfloat16)
    return a, b, (rest - b.astype(F32)).astype(jnp.bfloat16)


def picked(terms, pick):
    return sum(jnp.dot(x, pick, preferred_element_type=F32) for x in terms)


def slide(slot, patterns):
    slot[...] = jnp.zeros(slot.shape, F32)
    p, lane = iota((TILE, COLS), 0), iota((TILE, COLS), 1)
    for i, moves in enumerate(patterns):
        hit = jnp.zeros((TILE, COLS), F32)
        for to, sources in moves.items():
            for source in sources:
                hit = jnp.where((lane == to) & (p == source), 1.0, hit)
        slot[120:128, COLS * i:COLS * i + COLS] = hit


def slid(slot, k):
    return slot[120 - 8 * k:248 - 8 * k, :].astype(jnp.bfloat16)


AROUND = {126: (0,), 127: (1,), 0: (2,), 1: (3,)}
NEXT1 = {127: (1,), 0: (6,)}
OWN1 = {0: (2,), 127: (5,)}
THIRD = {1: 0, 2: 3, 5: 4, 6: 7}


def with_third(moves):
    return {to: (p, THIRD[p]) for to, (p,) in moves.items()}


def rows_at(b):
    return pl.multiple_of(b * TILE + PAD, TILE)


def pack_kernel(place, t, s, u, v, flag, tally, col_p, col_q, own_cols, rows, wet, t_in, s_in, u_in, v_in, open_e,
                link, spin, held_flag, held_tally, sems, gathered):
    field = (t_in, s_in, u_in, v_in)
    odd = place[1] % 2 == 1
    lane = iota((TILE, COLS), 1)
    sub = iota((TILE, COLS), 0)
    group = jnp.where(lane % 8 < 4, lane // 8, -1)
    inside = pl.ds(PAD, ROWS)
    copies = [pltpu.make_async_copy(x, field[f].at[:, inside, :], sems.at[f]) for f, x in enumerate((t, s, u, v))]
    copies.append(pltpu.make_async_copy(flag, held_flag, sems.at[4]))
    copies.append(pltpu.make_async_copy(tally, held_tally, sems.at[5]))
    for f in (4, 5, 0, 1, 2, 3):
        copies[f].start()
    copies[4].wait()
    copies[5].wait()

    def face_block(b, carry):
        here = pl.ds(rows_at(b), TILE)
        src = pl.ds(pl.multiple_of(b * TILE, TILE), TILE)
        deep = held_tally[src, :]
        column = [jnp.where(k < deep, held_flag[k, src, :], 0).astype(F32) for k in range(LEVELS)]
        for k, w in enumerate(column):
            wet[k, here, :] = w
            open_e[k, src, :] = w * roll(w, COLS - 1, 1)
        for k, (up, inverse, ratio) in enumerate(links_of(column)):
            if up is not None:
                link[0, k, src, :] = up
            link[1, k, src, :] = inverse
            if ratio is not None:
                link[2, k, src, :] = ratio
        row = (place[0] * ROWS + b * TILE + iota((TILE, COLS), 0)).astype(F32)
        spin[src, :] = spin_of(row)
        return carry

    lax.fori_loop(0, BLOCKS, face_block, 0, unroll=3)
    for f in (4, 0, 1, 2, 3):
        if f < STATE:
            copies[f].wait()
        for b in range(BLOCKS):
            at = PAD + TILE * b
            out = jnp.zeros((TILE, COLS), F32)
            for k in range(LEVELS):
                x = (field[f] if f < STATE else wet)[k, at:at + TILE, :]
                out = jnp.where(group == k, roll(x, 8 * k + 2, 1), out)
            gathered[f, TILE * b:TILE * b + TILE, :] = out
        gathered[f, ROWS:COLS, :] = jnp.zeros((COLS - ROWS, COLS), F32)
    for f in range(FIELDS):
        own_cols[f] = gathered[f].T
    for side, first in ((0, PAD), (1, PAD + ROWS - 2)):
        for m in range(LEVELS + 4):
            parts = []
            for i in range(4):
                at = first - 2 * i
                if m < LEVELS:
                    parts.append(field[i][m, at:at + TILE, :])
                else:
                    k = min(4 * (m - LEVELS) + i, LEVELS - 1)
                    parts.append(wet[k, at:at + TILE, :])
            rows[side, TILE * m:TILE * m + TILE, :] = jnp.where(
                sub < 2, parts[0], jnp.where(sub < 4, parts[1], jnp.where(sub < 6, parts[2], parts[3])))
    for f in range(FIELDS):
        for c in range(2):
            last = own_cols[f, pl.ds(c, 16, stride=8), :]
            first = own_cols[f, pl.ds(2 + c, 16, stride=8), :]
            at = (2 * f + c) * 16
            col_p[at:at + 16, :] = jnp.where(odd, first, last)
            col_q[at:at + 16, :] = jnp.where(odd, last, first)


def spread_kernel(place, got_p, got_q, own_cols, rows, _, strip, ghost, own, to_x, to_y, turned):
    odd = place[1] % 2 == 1
    lat_odd = place[0] % 2 == 1
    fold = place[0] == 7
    for f in range(FIELDS):
        for c in range(2):
            at = (2 * f + c) * 16
            a, b = got_p[at:at + 16, :], got_q[at:at + 16, :]
            west, east = jnp.where(odd, a, b), jnp.where(odd, b, a)
            strip[f, pl.ds(c, 16, stride=8), :] = west
            strip[f, pl.ds(6 + c, 16, stride=8), :] = east
            strip[f, pl.ds(2 + c, 16, stride=8), :] = own_cols[f, pl.ds(2 + c, 16, stride=8), :]
            strip[f, pl.ds(4 + c, 16, stride=8), :] = own_cols[f, pl.ds(c, 16, stride=8), :]
            turned[f, pl.ds(c, 16, stride=8), :] = west
            turned[f, pl.ds(2 + c, 16, stride=8), :] = east
            turned[f, pl.ds(4 + c, 16, stride=8), :] = west
            turned[f, pl.ds(6 + c, 16, stride=8), :] = east
    for f in range(FIELDS):
        ghost[f] = turned[f].T
    for f in range(FIELDS):
        own[0, EDGE_AT + 2 * f:EDGE_AT + 2 * f + 2, :] = ghost[f, 0:2, :]
        own[1, EDGE_AT + 2 * f:EDGE_AT + 2 * f + 2, :] = ghost[f, ROWS - 2:ROWS, :]
    for side in range(2):
        own[side, 0:EDGE_AT, :] = rows[side]
        own[side, EDGE_AT + 2 * FIELDS:MESSAGE, :] = jnp.zeros((MESSAGE - EDGE_AT - 2 * FIELDS, COLS), F32)
    low, high = own[0], own[1]
    to_x[...] = jnp.where(lat_odd, high, low)
    to_y[...] = jnp.where(lat_odd, low, high)

    @pl.when(fold)
    def _():
        a, b = iota((COLS, COLS), 0), iota((COLS, COLS), 1)
        mirror = (a + b == COLS - 1).astype(jnp.bfloat16)
        mirror_edge = ((a // 8 == b // 8) & (a % 8 < 4) & (a % 8 + b % 8 == 3)).astype(jnp.bfloat16)
        to_x[0:EDGE_AT, :] = picked(split3(own[1, 0:EDGE_AT, :]), mirror)
        to_x[EDGE_AT:MESSAGE, :] = picked(split3(own[1, EDGE_AT:MESSAGE, :]), mirror_edge)


def first_kernel(t, s, u, v, wet, open_e, link, spin, field1, flux):
    field = (t, s, u, v)

    def step_block(b, carry):
        r = rows_at(b)
        src = pl.ds(pl.multiple_of(b * TILE, TILE), TILE)

        def get(f, k, dj, di):
            x = field[f][k, pl.ds(r + dj, TILE), :]
            return roll(x, -di, 1) if di else x

        def faces(k):
            w = wet[k, pl.ds(r, TILE), :]
            return (w, open_e[k, src, :], None, w * wet[k, pl.ds(r + 1, TILE), :], None)

        def south(f, k, x):
            flux[f, k, pl.ds(r, TILE), :] = x
            return flux[f, k, pl.ds(r - 1, TILE), :]

        moved = column_step(get, faces, lambda k: tuple(link[i, k, src, :] for i in range(3)), spin[src, :],
                            lambda f, k, x: roll(x, 1, 1), south)
        for f in range(STATE):
            for k in range(LEVELS):
                field1[f, k, pl.ds(r, TILE), :] = moved[f][k]
        return carry

    lax.fori_loop(0, BLOCKS, step_block, 0, unroll=4)


def second_kernel(place, field1, wet, open_e, link, spin, strip, ghost, t, s, u, v, inner, inner_ghost, blocks,
                  state, outs, ghost1, turned, beside, face, flux, slot, slot_third, terms, sems):
    first_row = place[0] * ROWS
    lane = iota((TILE, COLS), 1)
    sub = iota((TILE, COLS), 0)

    def strip_shift(x, dj, di):
        if di:
            x = roll(x, -di, 0)
        return roll(x, -dj, 1) if dj else x

    values = [[strip[f, 8 * k:8 * k + 8, :] for k in range(LEVELS)] for f in range(FIELDS)]
    get1 = eager(strip_shift, values)
    row = (first_row + iota((1, COLS), 1)).astype(F32)
    links1 = links_of(values[4])
    moved = column_step(get1, faces_of(get1), lambda k: links1[k], spin_of(row))
    for f in range(STATE):
        for k in range(LEVELS):
            turned[f, 8 * k:8 * k + 8, :] = moved[f][k]
    faces1 = faces_of(get1)
    for f in range(2):
        for k in range(LEVELS):
            c, speed, face_e = moved[f][k], moved[2][k], faces1(k)[1]
            low = jnp.maximum(speed, 0.0) + KAPPA
            turned[STATE + f, 8 * k:8 * k + 8, :] = roll(face_e * (low * c - (low - speed) * roll(c, -1, 0)), 5, 0)
    for k in range(LEVELS):
        w = values[4][k]
        turned[GROUPS - 1, 8 * k:8 * k + 8, :] = jnp.where(sub == 2, roll(w, 1, 0), roll(w, -1, 0))
    for g in range(GROUPS):
        turned[g, 8 * LEVELS:COLS, :] = jnp.zeros((COLS - 8 * LEVELS, COLS), F32)
    for g in range(GROUPS):
        ghost1[g] = turned[g].T

    inside = pl.ds(PAD, ROWS)
    wide = iota((ROWS, COLS), 1)
    edge_lane = (wide == 0) | (wide == COLS - 1)
    place_in = wide % 8
    second = (place_in == 1) | (place_in == 2) | (place_in == 5) | (place_in == 6)
    from_east = (place_in == 0) | (place_in == 4)
    slide(slot, (NEXT1, OWN1))
    slide(slot_third, (with_third(NEXT1), with_third(OWN1)))
    for g in range(GROUPS):
        x = ghost1[g, 0:ROWS, :]
        a = x.astype(jnp.bfloat16)
        rest = x - a.astype(F32)
        b = rest.astype(jnp.bfloat16).astype(F32)
        c = rest - b
        terms[ROWS * g:ROWS * g + ROWS, 0:COLS] = a
        terms[ROWS * g:ROWS * g + ROWS, COLS:2 * COLS] = jnp.where(
            second, b, jnp.where(from_east, roll(c, -1, 1), roll(c, 1, 1))).astype(jnp.bfloat16)
    for k in range(LEVELS):
        pick = jnp.concatenate([slid(slot, k), slid(slot_third, k)], axis=0)
        found = jnp.dot(terms[...], pick, preferred_element_type=F32)
        face[k] = found[ROWS * (GROUPS - 1):, COLS:]
        for f in range(STATE + 2):
            beside[f, k, inside, :] = found[ROWS * f:ROWS * f + ROWS, :COLS]
        for f in range(STATE):
            state[f, k, inside, :] = jnp.where(edge_lane, found[ROWS * f:ROWS * f + ROWS, COLS:], field1[f, k, inside, :])

    def copies(b):
        src = pl.ds(pl.multiple_of(b * TILE, TILE), TILE)
        return [pltpu.make_async_copy(outs.at[f, :, src, :], x.at[:, src, :], sems.at[f, b])
                for f, x in enumerate((t, s, u, v))]

    def step_block(b, carry):
        r = rows_at(b)
        src = pl.ds(pl.multiple_of(b * TILE, TILE), TILE)

        def get(f, k, dj, di):
            here = pl.ds(r + dj, TILE)
            x = state[f, k, here, :]
            if di == 0:
                return x
            return roll(jnp.where(lane == (0 if di > 0 else COLS - 1), beside[f, k, here, :], x), -di, 1)

        def faces(k):
            w = wet[k, pl.ds(r, TILE), :]
            across = w * face[k, src, :]
            return (w, jnp.where(lane == COLS - 1, across, open_e[k, src, :]), None,
                    w * wet[k, pl.ds(r + 1, TILE), :], None)

        def west(f, k, x):
            return jnp.where(lane == 0, beside[STATE + f, k, pl.ds(r, TILE), :], roll(x, 1, 1))

        def south(f, k, x):
            flux[f, k, pl.ds(r, TILE), :] = x
            return flux[f, k, pl.ds(r - 1, TILE), :]

        moved = column_step(get, faces, lambda k: tuple(link[i, k, src, :] for i in range(3)), spin[src, :], west, south)
        for f in range(STATE):
            for k in range(LEVELS):
                outs[f, k, src, :] = moved[f][k]
        @pl.when((b > 0) & (b < BLOCKS - 1))
        def _():
            for c in copies(b):
                c.start()

        return carry

    lax.fori_loop(0, BLOCKS, step_block, 0, unroll=4)

    for f in range(FIELDS):
        for k in range(LEVELS):
            src = state.at[f, k] if f < STATE else wet.at[k]
            inner[f, k] = jnp.where(sub < 4, src[PAD - 1:PAD + 7, :], src[PAD + 89:PAD + 97, :])
        edge = ghost1.at[f] if f < STATE else ghost.at[4]
        inner_ghost[f] = jnp.where(sub < 4, roll(edge[0:8, :], 1, 0), edge[89:97, :])
    for f in range(STATE):
        for side, first in ((0, 0), (1, ROWS - TILE)):
            blocks[side, f] = outs[f, :, first:first + TILE, :]

    def drain(b, carry):
        for c in copies(b):
            c.wait()
        return carry

    lax.fori_loop(1, BLOCKS - 1, drain, 0)


def edge_kernel(place, own, got_x, got_y, inner, inner_ghost, blocks, t, s, u, v, t_out, s_out, u_out, v_out,
                low, high, mine_low, mine_high, slot, ring, lead, moved1, ring2, lead2, final, sems):
    lat = place[0]
    odd = lat % 2 == 1
    fold = lat == 7
    sub = iota((TILE, COLS), 0)
    lane = iota((TILE, COLS), 1)
    tile = slice(PAD, PAD + TILE)
    body_rows = slice(PAD, PAD + MESSAGE)
    from_x, from_y = got_x[...], got_y[...]
    low[body_rows, :] = jnp.where(odd, from_y, jnp.where(lat == 0, 0.0, from_x))
    high[body_rows, :] = jnp.where(odd, from_x, from_y)
    mine_low[body_rows, :] = own[0]
    mine_high[body_rows, :] = own[1]
    slide(slot, (AROUND, NEXT1))

    def rows(ref, at, early):
        return ref[PAD + at - early:PAD + at - early + TILE, :]

    def where_of(f, k):
        return 8 * k + 2 * f if f < STATE else WET_AT + 2 * k

    def stack(at, sign):
        top = jnp.where(fold, sign * rows(high, at, 5), rows(high, at, 6))
        return jnp.where(sub < 2, rows(low, at, 0), jnp.where(
            sub < 4, rows(mine_low, at, 2), jnp.where(sub < 6, rows(mine_high, at, 4), top)))

    def stack_fold(at, sign):
        return jnp.where(sub < 2, rows(high, at, 0), sign * rows(mine_high, at, 1))

    def spreads(tiles):
        terms = split3(jnp.concatenate(tiles, axis=0))
        out = []
        for k in range(LEVELS):
            found = picked(terms, slid(slot, k))
            out.append([(found[TILE * i:TILE * i + TILE, :COLS], found[TILE * i:TILE * i + TILE, COLS:])
                        for i in range(len(tiles))])
        return out

    def ring_getter(build, edges, back):
        held = {}
        for f in range(FIELDS):
            for k in range(LEVELS):
                x, g = build(where_of(f, k), SIGNS[f]), edges[k][f][0]
                ring[f, k, tile, :COLS] = x
                ring[f, k, tile, COLS:] = g
                held[f, k, 0, 0] = (x, g)
        for f in range(FIELDS):
            for k in range(LEVELS):
                x, g = held[f, k, 0, 0]
                a, b = jnp.where(lane == 0, g, x), jnp.where(lane == 0, x, g)
                held[f, k, 0, back] = (roll(a, -1, 1), roll(b, -1, 1))
                a, b = jnp.where(lane == COLS - 1, g, x), jnp.where(lane == COLS - 1, x, g)
                held[f, k, 0, -back] = (roll(a, 1, 1), roll(b, 1, 1))
        for f, di in ((2, -1), (3, 1)):
            for k in range(LEVELS):
                x, g = held[f, k, 0, di]
                lead[f - 2, k, tile, :COLS] = x
                lead[f - 2, k, tile, COLS:] = g

        def get(f, k, dj, di):
            if dj == 0:
                return jnp.concatenate(held[f, k, 0, di], axis=1)
            ref = lead.at[f - 2, k] if di else ring.at[f, k]
            return ref[PAD + dj:PAD + dj + TILE, :]

        return get

    def one_step(get, row):
        links = links_of([get(4, k, 0, 0) for k in range(LEVELS)])
        return column_step(get, faces_of(get), lambda k: links[k], spin_of(row))

    def global_rows(low_row, high_row):
        i = iota((TILE, 1), 0)
        return (lat * ROWS + i + jnp.where(i < 4, low_row, high_row - 4)).astype(F32)

    near_tiles = [inner_ghost[f] for f in range(FIELDS)]
    placed = spreads([stack(EDGE_AT + 2 * f, SIGNS[f]) for f in range(FIELDS)] + near_tiles)
    first = one_step(ring_getter(stack, placed, 1), global_rows(-2, ROWS - 2))
    for f in range(STATE):
        for k in range(LEVELS):
            moved1[f, k, tile, :] = first[f][k]
    for k in range(LEVELS):
        moved1[STATE, k, tile, :] = ring[STATE, k, tile, :]

    @pl.when(fold)
    def _():
        edges = spreads([stack_fold(EDGE_AT + 2 * f, SIGNS[f]) for f in range(FIELDS)])
        row = jnp.full((TILE, 1), 8.0 * ROWS - 1.0, F32)
        mirror = one_step(ring_getter(stack_fold, edges, -1), row)
        wide = iota((TILE, 2 * COLS), 0)
        for f in range(STATE):
            for k in range(LEVELS):
                ring[f, k, tile, :] = mirror[f][k]
        for f in range(STATE):
            for k in range(LEVELS):
                moved1[f, k, tile, :] = jnp.where(
                    wide == 6, SIGNS[f] * ring[f, k, PAD - 5:PAD + 3, :], moved1[f, k, tile, :])

    held = {}
    ghosts = {}
    for f in range(FIELDS):
        for k in range(LEVELS):
            down, up = moved1[f, k, PAD + 1:PAD + 1 + TILE, :], moved1[f, k, PAD - 1:PAD - 1 + TILE, :]
            near = placed[k][FIELDS + f][1 if f < STATE else 0]
            both = [jnp.where(sub < 2, down[:, c], jnp.where(sub < 6, mid, up[:, c]))
                    for c, mid in ((slice(0, COLS), inner[f, k]), (slice(COLS, 2 * COLS), near))]
            held[f, k, 0, 0], ghosts[f, k] = both
            ring2[f, k, tile, :] = both[0]
    for f in range(FIELDS):
        for k in range(LEVELS):
            x, g = held[f, k, 0, 0], ghosts[f, k]
            held[f, k, 0, 1] = roll(jnp.where(lane == 0, g, x), -1, 1)
            held[f, k, 0, -1] = roll(jnp.where(lane == COLS - 1, g, x), 1, 1)
    for f, di in ((2, -1), (3, 1)):
        for k in range(LEVELS):
            lead2[f - 2, k, tile, :] = held[f, k, 0, di]

    def get2(f, k, dj, di):
        if dj == 0:
            return held[f, k, 0, di]
        ref = lead2.at[f - 2, k] if di else ring2.at[f, k]
        return ref[PAD + dj:PAD + dj + TILE, :]

    last = one_step(get2, global_rows(-1, ROWS - 3))
    for f in range(STATE):
        for k in range(LEVELS):
            ring2[f, k, tile, :] = last[f][k]
    for f in range(STATE):
        for k in range(LEVELS):
            final[0, f, k] = jnp.where(sub < 2, ring2[f, k, PAD + 1:PAD + 1 + TILE, :], blocks[0, f, k])
            final[1, f, k] = jnp.where(sub >= 6, ring2[f, k, PAD - 1:PAD - 1 + TILE, :], blocks[1, f, k])
    copies = [pltpu.make_async_copy(final.at[side, f], x.at[:, first_row:first_row + TILE, :], sems.at[side, f])
              for f, x in enumerate((t_out, s_out, u_out, v_out)) for side, first_row in ((0, 0), (1, ROWS - TILE))]
    for c in copies:
        c.start()
    for c in copies:
        c.wait()


def limit(mebibytes):
    return pltpu.CompilerParams(vmem_limit_bytes=mebibytes * 1024 * 1024)


def call(kernel, place, args, outs, scratch, mebibytes, flops, far_in=0, far_out=0, handed_on=0):
    far = [i < far_in or i >= len(args) - handed_on for i in range(len(args))]
    vmem, hbm = pl.BlockSpec(memory_space=pltpu.VMEM), pl.BlockSpec(memory_space=pltpu.HBM)
    args = [pltpu.with_memory_space_constraint(a, pltpu.HBM if there else pltpu.VMEM) for a, there in zip(args, far)]
    return pl.pallas_call(
        kernel,
        out_shape=[jax.ShapeDtypeStruct(o, F32) if i < far_out else pltpu.VMEM(o, F32) for i, o in enumerate(outs)],
        in_specs=[pl.BlockSpec(memory_space=pltpu.SMEM)] + [hbm if there else vmem for there in far],
        out_specs=[hbm if i < far_out else vmem for i in range(len(outs))],
        scratch_shapes=[pltpu.VMEM(x, F32) if isinstance(x, tuple) else x for x in scratch],
        input_output_aliases={1 + len(args) - handed_on + i: i for i in range(handed_on)},
        compiler_params=limit(mebibytes),
        cost_estimate=pl.CostEstimate(flops=flops, bytes_accessed=4_000_000, transcendentals=0),
    )(place, *args)


def device(lon, lat, lats, lons):
    return lon % lons * lats + lat


def body(t, s, u, v, flag, tally):
    lons, lats = lax.axis_size("lon"), lax.axis_size("lat")
    lat, lon = lax.axis_index("lat"), lax.axis_index("lon")
    place = jnp.stack([lat, lon]).astype(jnp.int32)
    pairs_p, pairs_q, pairs_x, pairs_y = [], [], [], []
    for a in range(lats):
        for o in range(lons):
            here = device(o, a, lats, lons)
            pairs_p.append((here, device(o ^ 1, a, lats, lons)))
            pairs_q.append((here, device(o + 1 if o % 2 else o - 1, a, lats, lons)))
            pairs_y.append((here, device(o, a ^ 1, lats, lons)))
            next_lat = a + 1 if a % 2 else a - 1
            inside = 0 <= next_lat < lats
            pairs_x.append((here, device(o, next_lat, lats, lons) if inside else device(lons - 1 - o, a, lats, lons)))

    def send(x, pairs):
        return lax.ppermute(x, ("lon", "lat"), pairs)

    edges = (2, STATE, LEVELS, TILE, COLS)
    deep, tall, square = (LEVELS, ROWS, COLS), (LEVELS, TALL, COLS), (FIELDS, COLS, COLS)
    message = (MESSAGE, COLS)
    col_p, col_q, own_cols, rows, wet, *padded, open_e, link, spin = call(
        pack_kernel, place, (t, s, u, v, flag, tally), [(PACK, COLS), (PACK, COLS), square, (2, EDGE_AT, COLS)] + [tall] * 5
        + [deep, (3,) + deep, (ROWS, COLS)], [pltpu.VMEM(deep, jnp.int32), pltpu.VMEM((ROWS, COLS), jnp.int32), pltpu.SemaphoreType.DMA((6,)), square],
        12, 1_000_000, far_in=6)
    got_p, got_q = send(col_p, pairs_p), send(col_q, pairs_q)
    field1, = call(lambda _, *refs: first_kernel(*refs), place, (*padded, wet, open_e, link, spin), [(STATE,) + tall],
                   [(2,) + tall], 12, 40_000_000)
    strip, ghost, own, to_x, to_y = call(
        spread_kernel, place, (got_p, got_q, own_cols, rows, field1), [square, square, (2, MESSAGE, COLS), message, message],
        [square], 4, 1_000_000)
    got_x, got_y = send(to_x, pairs_x), send(to_y, pairs_y)
    *fields, inner, inner_ghost, blocks = call(
        second_kernel, place, (field1, wet, open_e, link, spin, strip, ghost),
        [deep] * STATE + [(FIELDS, LEVELS, TILE, COLS), (FIELDS, TILE, COLS), edges],
        [(STATE,) + tall, (STATE,) + deep, (GROUPS, COLS, COLS), (GROUPS, COLS, COLS), (STATE + 2,) + tall, deep,
         (2,) + tall, (248, 2 * COLS), (248, 2 * COLS), pltpu.VMEM((GROUPS * ROWS, 2 * COLS), jnp.bfloat16),
         pltpu.SemaphoreType.DMA((STATE, BLOCKS))], 20, 50_000_000, far_out=STATE)
    near, wide = (FIELDS, LEVELS, 3 * TILE, COLS), (FIELDS, LEVELS, 3 * TILE, 2 * COLS)
    padded = (MESSAGE + 2 * PAD, COLS)
    return tuple(call(
        edge_kernel, place, (own, got_x, got_y, inner, inner_ghost, blocks, *fields), [deep] * STATE,
        [padded] * 4 + [(248, 2 * COLS), wide, (2,) + wide[1:], wide, near, (2,) + near[1:], edges,
                        pltpu.SemaphoreType.DMA((2, STATE))], 16, 2_000_000, far_out=STATE, handed_on=STATE))


def solution(mesh):
    cut = P(None, "lat", "lon")
    return jax.shard_map(
        body,
        mesh=mesh,
        in_specs=(cut, cut, cut, cut, cut, P("lat", "lon")),
        out_specs=(cut, cut, cut, cut),
        check_vma=False,
    )
```

time: 38.9 us -> 31.5 us (0.81)
  the two profiles are of different devices: /device:TPU:8 before, /device:TPU:24 now
where the time goes in v2:
time: 31.5 us; the launch traced here: 31.4 us
  Pallas kernels  18.5 us (59%)
  starting transfers between devices  12.1 us (38%)
  between operations  0.7 us (2%)
    pallas_call x5, Pallas kernels, call(): pl.pallas_call(kernel, out_shape=[jax.ShapeDtypeStruct(o, F32) if i < far...  18.5 us
    ppermute x4, starting transfers between devices, send(): return lax.ppermute(x, ('lon', 'lat'), pairs)  12.1 us
  transfers between devices with their start and end apart: 4, of which 0 were waited for; matrix products, arithmetic and copies ran while one was open for 0% of the time, Pallas kernels for 34%

profile of v2, /device:TPU:24, one launch (start us, length us, event | category | flops | bytes accessed | tf_op | source)
XLA Modules:
  0.0 31.4 jit_solution(16345115839944927542)
XLA Ops:
  0.6 0.1 pad_add_fusion.place._
  0.7 4.0 %shard_map.93 = (f32[160,128]{1,0:T(8,128)S(1)}, f32[160,128]{1,0:T(8,128)S(1)}, f32[5,128,128]{2,1,0:T(8,128)S(1)}, f32[2,152,128]{2,1,0:T(8,128)S(1)}, f32[15,...) custom-call(s32[2]{0:T(128)S(1)} %pad_add_fusion.place._, ...), custom_call_target="tpu_custom_call" | custom-call | flops 1000000 | bytes 4000000 | tf_op jit(solution)/shard_map/pallas_call | solution.py:594
  4.7 0.1 collective-permute-start
  4.8 6.9 %collective-permute-start.1 = (f32[160,128]{1,0:T(8,128)S(1)}, f32[160,128]{1,0:T(8,128)S(1)}, u32[]{:S(2)}, u32[]{:S(2)}) collective-permute-start(f32[160,128]{1,0:T(8,128)S(1)} %get-tuple-element.29), channel_id=1, source_target_pairs={{0,248},{8,16},{16,8},{24,32},{32,24},{40,48},{48,40},{56,64},{64,... | collective-permute-start | bytes 245768 | tf_op jit(solution)/shard_map/ppermute | solution.py:626
  11.7 3.8 %shard_map.94._.field1 = f32[4,15,112,128]{3,2,1,0:T(8,128)S(1)} custom-call(s32[2]{0:T(128)S(1)} %pad_add_fusion.place._, f32[15,112,128]{2,1,0:T(8,128)S(1)} %get-tuple-element.32.refs_0_, f32[15,112,128]{2,1,0:T(8,128)S(1)} %get-tuple-element.33.refs_1_, f32[15,112,128]{2,1,0:T(8,128)S(1)} %get-tuple-element.34.refs_2_, ...), custom_call_target="tpu_custom_call" | custom-call | flops 40000000 | bytes 4000000 | tf_op jit(solution)/shard_map/pallas_call | solution.py:594
  15.5 0.0 collective-permute-done.got_p
  15.5 0.0 collective-permute-done.1.got_q
  15.5 0.8 %shard_map.95 = (f32[5,128,128]{2,1,0:T(8,128)S(1)}, f32[5,128,128]{2,1,0:T(8,128)S(1)}, f32[2,168,128]{2,1,0:T(8,128)S(1)}, f32[168,128]{1,0:T(8,128)S(1)}, f32[168,128]{1,0:T(8,128)S(1)}) custom-call(s32[2]{0:T(128)S(1)} %pad_add_fusion.place._, f32[160,128]{1,0:T(8,128)S(1)} %collective-permute-done.got_p, f32[160,128]{1,0:T(8,128)S(1)} %collective-permute-done.1.got_q, ...), custom_call_target="tpu_custom_call" | custom-call | flops 1000000 | bytes 4000000 | tf_op jit(solution)/shard_map/pallas_call | solution.py:594
  16.3 3.0 %collective-permute-start.2 = (f32[168,128]{1,0:T(8,128)S(1)}, f32[168,128]{1,0:T(8,128)S(1)}, u32[]{:S(2)}, u32[]{:S(2)}) collective-permute-start(f32[168,128]{1,0:T(8,128)S(1)} %get-tuple-element.41), channel_id=1, source_target_pairs={{0,248},{8,240},{16,232},{24,224},{32,216},{40,208},{48,200},{56,1... | collective-permute-start | bytes 258056 | tf_op jit(solution)/shard_map/ppermute | solution.py:626
  19.3 2.2 %collective-permute-start.3 = (f32[168,128]{1,0:T(8,128)S(1)}, f32[168,128]{1,0:T(8,128)S(1)}, u32[]{:S(2)}, u32[]{:S(2)}) collective-permute-start(f32[168,128]{1,0:T(8,128)S(1)} %get-tuple-element.42), channel_id=1, source_target_pairs={{0,1},{8,9},{16,17},{24,25},{32,33},{40,41},{48,49},{56,57},{64,65... | collective-permute-start | bytes 258056 | tf_op jit(solution)/shard_map/ppermute | solution.py:626
  21.5 6.8 %shard_map.96 = (f32[15,96,128]{2,1,0:T(8,128)}, f32[15,96,128]{2,1,0:T(8,128)}, f32[15,96,128]{2,1,0:T(8,128)}, f32[15,96,128]{2,1,0:T(8,128)}, f32[5,15,8,128]...) custom-call(s32[2]{0:T(128)S(1)} %pad_add_fusion.place._, ...), custom_call_target="tpu_custom_call" | custom-call | flops 50000000 | bytes 4000000 | tf_op jit(solution)/shard_map/pallas_call | solution.py:594
  28.3 0.0 collective-permute-done.2.got_x
  28.3 0.0 collective-permute-done.3.got_y
  28.3 3.1 %shard_map.97 = (f32[15,96,128]{2,1,0:T(8,128)}, f32[15,96,128]{2,1,0:T(8,128)}, f32[15,96,128]{2,1,0:T(8,128)}, f32[15,96,128]{2,1,0:T(8,128)}) custom-call(s32[2]{0:T(128)S(1)} %pad_add_fusion.place._, f32[2,168,128]{2,1,0:T(8,128)S(1)} %get-tuple-element.40.own, ...), custom_call_target="tpu_custom_call", output_to_operand_aliasing={{0}: (7, {}), {1}: (8, {}), {2}: (9, {}), {3}: (10, {})} | custom-call | flops 2000000 | bytes 4000000 | tf_op jit(solution)/shard_map/pallas_call | solution.py:594
Async XLA Ops:
  4.7 10.8 %collective-permute-start = (f32[160,128]{1,0:T(8,128)S(1)}, f32[160,128]{1,0:T(8,128)S(1)}, u32[]{:S(2)}, u32[]{:S(2)}) collective-permute-start(f32[160,128]{1,0:T(8,128)S(1)} %get-tuple-element.28), channel_id=1, source_target_pairs={{0,8},{8,0},{16,24},{24,16},{32,40},{40,32},{48,56},{56,48},{64,72... | collective-permute-start | bytes 245768 | tf_op jit(solution)/shard_map/ppermute | solution.py:626
  4.8 10.7 %collective-permute-start.1 = (f32[160,128]{1,0:T(8,128)S(1)}, f32[160,128]{1,0:T(8,128)S(1)}, u32[]{:S(2)}, u32[]{:S(2)}) collective-permute-start(f32[160,128]{1,0:T(8,128)S(1)} %get-tuple-element.29), channel_id=1, source_target_pairs={{0,248},{8,16},{16,8},{24,32},{32,24},{40,48},{48,40},{56,64},{64,... | collective-permute-start | bytes 245768 | tf_op jit(solution)/shard_map/ppermute | solution.py:626
  16.3 12.0 %collective-permute-start.2 = (f32[168,128]{1,0:T(8,128)S(1)}, f32[168,128]{1,0:T(8,128)S(1)}, u32[]{:S(2)}, u32[]{:S(2)}) collective-permute-start(f32[168,128]{1,0:T(8,128)S(1)} %get-tuple-element.41), channel_id=1, source_target_pairs={{0,248},{8,240},{16,232},{24,224},{32,216},{40,208},{48,200},{56,1... | collective-permute-start | bytes 258056 | tf_op jit(solution)/shard_map/ppermute | solution.py:626
  19.3 9.0 %collective-permute-start.3 = (f32[168,128]{1,0:T(8,128)S(1)}, f32[168,128]{1,0:T(8,128)S(1)}, u32[]{:S(2)}, u32[]{:S(2)}) collective-permute-start(f32[168,128]{1,0:T(8,128)S(1)} %get-tuple-element.42), channel_id=1, source_target_pairs={{0,1},{8,9},{16,17},{24,25},{32,33},{40,41},{48,49},{56,57},{64,65... | collective-permute-start | bytes 258056 | tf_op jit(solution)/shard_map/ppermute | solution.py:626

commit v3 on v2

--- a/solution.py
+++ b/solution.py
@@ -55,9 +55,10 @@
     return out
 
 
-def column_step(get, faces, links, spin, west=None, south=None):
+def column_step(get, faces, links, spin, west=None, south=None, early=None):
     mix = KAPPA
-    half = 0.5 * GRAVITY * TIME_STEP
+    half = 0.5 * GRAVITY
+    keep = (1.0 - 4.0 * TIME_STEP * VISCOSITY) / TIME_STEP
     done = [[], [], [], []]
     forward, loose = [], []
     east_sum = north_sum = None
@@ -82,7 +83,7 @@
                 out_e = out_e - (coef[1][0] * get(f, k, 0, -1) - coef[1][1] * c)
             out_n = coef[2][0] * c - coef[2][1] * cN
             out_s = south(f, k, out_n) if south else coef[3][0] * get(f, k, -1, 0) - coef[3][1] * c
-            tracers.append((c - TIME_STEP * (out_n - out_s), out_e))
+            tracers.append((c - (out_n - out_s), out_e))
             east.append(cE - c)
             north.append(cN - c)
         loose.append(tracers)
@@ -91,18 +92,19 @@
         east_p = east_now if k == 0 else east_sum + east_now
         north_p = north_now if k == 0 else north_sum + north_now
         east_sum, north_sum = east_p + east_now, north_p + north_now
-        turn = TIME_STEP * VISCOSITY
-        done[2].append(oe * ((1.0 - 4.0 * turn) * u + spin * ((v + vS) + (vE + vSE)) - east_p
-                             + turn * ((uE + uW) + (uN + uS))))
-        done[3].append(on * ((1.0 - 4.0 * turn) * v - spin * ((u + uN) + (uW + uNW)) - north_p
-                             + turn * ((vE + vW) + (vN + vS))))
+        done[2].append(oe * (keep * u + spin * ((v + vS) + (vE + vSE)) - east_p
+                             + VISCOSITY * ((uE + uW) + (uN + uS))))
+        done[3].append(on * (keep * v - spin * ((u + uN) + (uW + uNW)) - north_p
+                             + VISCOSITY * ((vE + vW) + (vN + vS))))
+    if early:
+        early(done)
     for k in range(LEVELS):
         w = faces(k)[0]
         up, inverse, _ = links(k)
         now = []
         for f in (0, 1):
             kept, out = loose[k][f]
-            x = w * (kept - TIME_STEP * (out - west(f, k, out) if west else out))
+            x = w * (kept - (out - west(f, k, out) if west else out))
             now.append((x + up * forward[-1][f]) * inverse if k else x * inverse)
         forward.append(now)
     for f in (0, 1):
@@ -117,7 +119,7 @@
 
 def spin_of(row_index):
     angle = jnp.pi * ((row_index + 0.5) / (8.0 * ROWS) - 0.3)
-    return (0.25 * TIME_STEP * CORIOLIS) * jnp.sin(angle)
+    return (0.25 * CORIOLIS) * jnp.sin(angle)
 
 
 SHIFTS = {0: (), 1: (), 2: (1, -1), 3: (-1, 1), 4: ()}
@@ -143,7 +145,8 @@
 def faces_of(get):
     def faces(k):
         w = get(4, k, 0, 0)
-        return (w, w * get(4, k, 0, 1), w * get(4, k, 0, -1), w * get(4, k, 1, 0), w * get(4, k, -1, 0))
+        long = TIME_STEP * w
+        return (w, long * get(4, k, 0, 1), long * get(4, k, 0, -1), long * get(4, k, 1, 0), long * get(4, k, -1, 0))
 
     return faces
 
@@ -182,10 +185,6 @@
 
 def with_third(moves):
     return {to: (p, THIRD[p]) for to, (p,) in moves.items()}
-
-
-def rows_at(b):
-    return pl.multiple_of(b * TILE + PAD, TILE)
 
 
 def pack_kernel(place, t, s, u, v, flag, tally, col_p, col_q, own_cols, rows, wet, t_in, s_in, u_in, v_in, open_e,
@@ -204,35 +203,40 @@
     copies[4].wait()
     copies[5].wait()
 
-    def face_block(b, carry):
-        here = pl.ds(rows_at(b), TILE)
-        src = pl.ds(pl.multiple_of(b * TILE, TILE), TILE)
-        deep = held_tally[src, :]
-        column = [jnp.where(k < deep, held_flag[k, src, :], 0).astype(F32) for k in range(LEVELS)]
+    def gather(f, b):
+        at = PAD + TILE * b
+        out = jnp.zeros((TILE, COLS), F32)
+        for k in range(LEVELS):
+            x = (field[f] if f < STATE else wet)[k, at:at + TILE, :]
+            out = jnp.where(group == k, roll(x, 8 * k + 2, 1), out)
+        gathered[f, TILE * b:TILE * b + TILE, :] = out
+
+    def couple(b):
+        here = slice(TILE * b, TILE * b + TILE)
+        column = [wet[k, PAD + TILE * b:PAD + TILE * b + TILE, :] for k in range(LEVELS)]
         for k, w in enumerate(column):
-            wet[k, here, :] = w
-            open_e[k, src, :] = w * roll(w, COLS - 1, 1)
+            open_e[k, here, :] = (TIME_STEP * w) * roll(w, COLS - 1, 1)
         for k, (up, inverse, ratio) in enumerate(links_of(column)):
             if up is not None:
-                link[0, k, src, :] = up
-            link[1, k, src, :] = inverse
+                link[0, k, here, :] = up
+            link[1, k, here, :] = inverse
             if ratio is not None:
-                link[2, k, src, :] = ratio
+                link[2, k, here, :] = ratio
         row = (place[0] * ROWS + b * TILE + iota((TILE, COLS), 0)).astype(F32)
-        spin[src, :] = spin_of(row)
-        return carry
-
-    lax.fori_loop(0, BLOCKS, face_block, 0, unroll=3)
+        spin[here, :] = spin_of(row)
+
+    for b in range(BLOCKS):
+        here = slice(TILE * b, TILE * b + TILE)
+        deep = held_tally[here, :]
+        for k in range(LEVELS):
+            wet[k, PAD + TILE * b:PAD + TILE * b + TILE, :] = jnp.where(k < deep, held_flag[k, here, :], 0).astype(F32)
     for f in (4, 0, 1, 2, 3):
         if f < STATE:
             copies[f].wait()
         for b in range(BLOCKS):
-            at = PAD + TILE * b
-            out = jnp.zeros((TILE, COLS), F32)
-            for k in range(LEVELS):
-                x = (field[f] if f < STATE else wet)[k, at:at + TILE, :]
-                out = jnp.where(group == k, roll(x, 8 * k + 2, 1), out)
-            gathered[f, TILE * b:TILE * b + TILE, :] = out
+            gather(f, b)
+            if f != 3 and b % 4 == 3:
+                couple(3 * (0 if f == 4 else f + 1) + b // 4)
         gathered[f, ROWS:COLS, :] = jnp.zeros((COLS - ROWS, COLS), F32)
     for f in range(FIELDS):
         own_cols[f] = gathered[f].T
@@ -298,30 +302,30 @@
 def first_kernel(t, s, u, v, wet, open_e, link, spin, field1, flux):
     field = (t, s, u, v)
 
-    def step_block(b, carry):
-        r = rows_at(b)
-        src = pl.ds(pl.multiple_of(b * TILE, TILE), TILE)
+    def step_block(b):
+        r = PAD + TILE * b
+        src = slice(TILE * b, TILE * b + TILE)
 
         def get(f, k, dj, di):
-            x = field[f][k, pl.ds(r + dj, TILE), :]
+            x = field[f][k, r + dj:r + dj + TILE, :]
             return roll(x, -di, 1) if di else x
 
         def faces(k):
-            w = wet[k, pl.ds(r, TILE), :]
-            return (w, open_e[k, src, :], None, w * wet[k, pl.ds(r + 1, TILE), :], None)
+            w = wet[k, r:r + TILE, :]
+            return (w, open_e[k, src, :], None, (TIME_STEP * w) * wet[k, r + 1:r + 1 + TILE, :], None)
 
         def south(f, k, x):
-            flux[f, k, pl.ds(r, TILE), :] = x
-            return flux[f, k, pl.ds(r - 1, TILE), :]
+            flux[f, k, r:r + TILE, :] = x
+            return flux[f, k, r - 1:r - 1 + TILE, :]
 
         moved = column_step(get, faces, lambda k: tuple(link[i, k, src, :] for i in range(3)), spin[src, :],
                             lambda f, k, x: roll(x, 1, 1), south)
         for f in range(STATE):
             for k in range(LEVELS):
-                field1[f, k, pl.ds(r, TILE), :] = moved[f][k]
-        return carry
-
-    lax.fori_loop(0, BLOCKS, step_block, 0, unroll=4)
+                field1[f, k, r:r + TILE, :] = moved[f][k]
+
+    for b in range(BLOCKS):
+        step_block(b)
 
 
 def second_kernel(place, field1, wet, open_e, link, spin, strip, ghost, t, s, u, v, inner, inner_ghost, blocks,
@@ -384,46 +388,47 @@
             state[f, k, inside, :] = jnp.where(edge_lane, found[ROWS * f:ROWS * f + ROWS, COLS:], field1[f, k, inside, :])
 
     def copies(b):
-        src = pl.ds(pl.multiple_of(b * TILE, TILE), TILE)
+        src = slice(TILE * b, TILE * b + TILE)
         return [pltpu.make_async_copy(outs.at[f, :, src, :], x.at[:, src, :], sems.at[f, b])
                 for f, x in enumerate((t, s, u, v))]
 
-    def step_block(b, carry):
-        r = rows_at(b)
-        src = pl.ds(pl.multiple_of(b * TILE, TILE), TILE)
+    def step_block(b):
+        r = PAD + TILE * b
+        src = slice(TILE * b, TILE * b + TILE)
 
         def get(f, k, dj, di):
-            here = pl.ds(r + dj, TILE)
+            here = slice(r + dj, r + dj + TILE)
             x = state[f, k, here, :]
             if di == 0:
                 return x
             return roll(jnp.where(lane == (0 if di > 0 else COLS - 1), beside[f, k, here, :], x), -di, 1)
 
         def faces(k):
-            w = wet[k, pl.ds(r, TILE), :]
-            across = w * face[k, src, :]
-            return (w, jnp.where(lane == COLS - 1, across, open_e[k, src, :]), None,
-                    w * wet[k, pl.ds(r + 1, TILE), :], None)
+            w = wet[k, r:r + TILE, :]
+            long = TIME_STEP * w
+            return (w, jnp.where(lane == COLS - 1, long * face[k, src, :], open_e[k, src, :]), None,
+                    long * wet[k, r + 1:r + 1 + TILE, :], None)
 
         def west(f, k, x):
-            return jnp.where(lane == 0, beside[STATE + f, k, pl.ds(r, TILE), :], roll(x, 1, 1))
+            return jnp.where(lane == 0, beside[STATE + f, k, r:r + TILE, :], roll(x, 1, 1))
 
         def south(f, k, x):
-            flux[f, k, pl.ds(r, TILE), :] = x
-            return flux[f, k, pl.ds(r - 1, TILE), :]
+            flux[f, k, r:r + TILE, :] = x
+            return flux[f, k, r - 1:r - 1 + TILE, :]
 
         moved = column_step(get, faces, lambda k: tuple(link[i, k, src, :] for i in range(3)), spin[src, :], west, south)
         for f in range(STATE):
             for k in range(LEVELS):
-                outs[f, k, src, :] = moved[f][k]
-        @pl.when((b > 0) & (b < BLOCKS - 1))
-        def _():
+                if 0 < b < BLOCKS - 1:
+                    outs[f, k, src, :] = moved[f][k]
+                else:
+                    blocks[b // (BLOCKS - 1), f, k] = moved[f][k]
+        if 0 < b < BLOCKS - 1:
             for c in copies(b):
                 c.start()
 
-        return carry
-
-    lax.fori_loop(0, BLOCKS, step_block, 0, unroll=4)
+    for b in range(BLOCKS):
+        step_block(b)
 
     for f in range(FIELDS):
         for k in range(LEVELS):
@@ -431,16 +436,9 @@
             inner[f, k] = jnp.where(sub < 4, src[PAD - 1:PAD + 7, :], src[PAD + 89:PAD + 97, :])
         edge = ghost1.at[f] if f < STATE else ghost.at[4]
         inner_ghost[f] = jnp.where(sub < 4, roll(edge[0:8, :], 1, 0), edge[89:97, :])
-    for f in range(STATE):
-        for side, first in ((0, 0), (1, ROWS - TILE)):
-            blocks[side, f] = outs[f, :, first:first + TILE, :]
-
-    def drain(b, carry):
+    for b in range(1, BLOCKS - 1):
         for c in copies(b):
             c.wait()
-        return carry
-
-    lax.fori_loop(1, BLOCKS - 1, drain, 0)
 
 
 def edge_kernel(place, own, got_x, got_y, inner, inner_ghost, blocks, t, s, u, v, t_out, s_out, u_out, v_out,
@@ -511,9 +509,9 @@
 
         return get
 
-    def one_step(get, row):
+    def one_step(get, row, early=None):
         links = links_of([get(4, k, 0, 0) for k in range(LEVELS)])
-        return column_step(get, faces_of(get), lambda k: links[k], spin_of(row))
+        return column_step(get, faces_of(get), lambda k: links[k], spin_of(row), early=early)
 
     def global_rows(low_row, high_row):
         i = iota((TILE, 1), 0)
@@ -567,19 +565,29 @@
         ref = lead2.at[f - 2, k] if di else ring2.at[f, k]
         return ref[PAD + dj:PAD + dj + TILE, :]
 
-    last = one_step(get2, global_rows(-1, ROWS - 3))
-    for f in range(STATE):
-        for k in range(LEVELS):
-            ring2[f, k, tile, :] = last[f][k]
-    for f in range(STATE):
+    def finish(f, levels):
+        for k in range(LEVELS):
+            ring2[f, k, tile, :] = levels[k]
         for k in range(LEVELS):
             final[0, f, k] = jnp.where(sub < 2, ring2[f, k, PAD + 1:PAD + 1 + TILE, :], blocks[0, f, k])
             final[1, f, k] = jnp.where(sub >= 6, ring2[f, k, PAD - 1:PAD - 1 + TILE, :], blocks[1, f, k])
-    copies = [pltpu.make_async_copy(final.at[side, f], x.at[:, first_row:first_row + TILE, :], sems.at[side, f])
-              for f, x in enumerate((t_out, s_out, u_out, v_out)) for side, first_row in ((0, 0), (1, ROWS - TILE))]
-    for c in copies:
-        c.start()
-    for c in copies:
+        x = (t_out, s_out, u_out, v_out)[f]
+        copies = [pltpu.make_async_copy(final.at[side, f], x.at[:, first_row:first_row + TILE, :], sems.at[side, f])
+                  for side, first_row in ((0, 0), (1, ROWS - TILE))]
+        for c in copies:
+            c.start()
+        return copies
+
+    flying = []
+
+    def early(done):
+        for f in (2, 3):
+            flying.extend(finish(f, done[f]))
+
+    last = one_step(get2, global_rows(-1, ROWS - 3), early)
+    for f in (0, 1):
+        flying.extend(finish(f, last[f]))
+    for c in flying:
         c.wait()
 
 

time: 31.5 us -> 30.8 us (0.978)
  Pallas kernels: 18.5 us -> 17.5 us
    pallas_call x5, Pallas kernels: 18.5 us -> 17.5 us  [call(): pl.pallas_call(kernel, out_shape=[jax.ShapeDtypeStruct(o, F32) if i < far...]
  transfers between devices with their start and end apart: 4 -> 4, of which waited for: 0 -> 0; matrix products, arithmetic and copies ran while one was open for 0% -> 0% of each run, Pallas kernels for 34% -> 33%
where the time goes in v3:
time: 30.8 us; the launch traced here: 30.7 us
  Pallas kernels  17.5 us (57%)
  starting transfers between devices  12.3 us (40%)
  between operations  0.86 us (3%)
    pallas_call x5, Pallas kernels, call(): pl.pallas_call(kernel, out_shape=[jax.ShapeDtypeStruct(o, F32) if i < far...  17.5 us
    ppermute x4, starting transfers between devices, send(): return lax.ppermute(x, ('lon', 'lat'), pairs)  12.3 us
  transfers between devices with their start and end apart: 4, of which 0 were waited for; matrix products, arithmetic and copies ran while one was open for 0% of the time, Pallas kernels for 33%

profile of v3, /device:TPU:24, one launch (start us, length us, event | category | flops | bytes accessed | tf_op | source)
XLA Modules:
  0.0 30.7 jit_solution(8087596159779728918)
XLA Ops:
  0.6 0.1 pad_add_fusion.place._
  0.7 3.4 %shard_map.93 = (f32[160,128]{1,0:T(8,128)S(1)}, f32[160,128]{1,0:T(8,128)S(1)}, f32[5,128,128]{2,1,0:T(8,128)S(1)}, f32[2,152,128]{2,1,0:T(8,128)S(1)}, f32[15,...) custom-call(s32[2]{0:T(128)S(1)} %pad_add_fusion.place._, ...), custom_call_target="tpu_custom_call" | custom-call | flops 1000000 | bytes 4000000 | tf_op jit(solution)/shard_map/pallas_call | solution.py:602
  4.1 0.1 collective-permute-start
  4.2 6.9 %collective-permute-start.1 = (f32[160,128]{1,0:T(8,128)S(1)}, f32[160,128]{1,0:T(8,128)S(1)}, u32[]{:S(2)}, u32[]{:S(2)}) collective-permute-start(f32[160,128]{1,0:T(8,128)S(1)} %get-tuple-element.29), channel_id=1, source_target_pairs={{0,248},{8,16},{16,8},{24,32},{32,24},{40,48},{48,40},{56,64},{64,... | collective-permute-start | bytes 245768 | tf_op jit(solution)/shard_map/ppermute | solution.py:634
  11.1 3.6 %shard_map.94._.field1 = f32[4,15,112,128]{3,2,1,0:T(8,128)S(1)} custom-call(s32[2]{0:T(128)S(1)} %pad_add_fusion.place._, f32[15,112,128]{2,1,0:T(8,128)S(1)} %get-tuple-element.32.refs_0_, f32[15,112,128]{2,1,0:T(8,128)S(1)} %get-tuple-element.33.refs_1_, f32[15,112,128]{2,1,0:T(8,128)S(1)} %get-tuple-element.34.refs_2_, ...), custom_call_target="tpu_custom_call" | custom-call | flops 40000000 | bytes 4000000 | tf_op jit(solution)/shard_map/pallas_call | solution.py:602
  14.7 0.0 collective-permute-done.got_p
  14.7 0.0 collective-permute-done.1.got_q
  14.8 0.8 %shard_map.95 = (f32[5,128,128]{2,1,0:T(8,128)S(1)}, f32[5,128,128]{2,1,0:T(8,128)S(1)}, f32[2,168,128]{2,1,0:T(8,128)S(1)}, f32[168,128]{1,0:T(8,128)S(1)}, f32[168,128]{1,0:T(8,128)S(1)}) custom-call(s32[2]{0:T(128)S(1)} %pad_add_fusion.place._, f32[160,128]{1,0:T(8,128)S(1)} %collective-permute-done.got_p, f32[160,128]{1,0:T(8,128)S(1)} %collective-permute-done.1.got_q, ...), custom_call_target="tpu_custom_call" | custom-call | flops 1000000 | bytes 4000000 | tf_op jit(solution)/shard_map/pallas_call | solution.py:602
  15.5 3.0 %collective-permute-start.2 = (f32[168,128]{1,0:T(8,128)S(1)}, f32[168,128]{1,0:T(8,128)S(1)}, u32[]{:S(2)}, u32[]{:S(2)}) collective-permute-start(f32[168,128]{1,0:T(8,128)S(1)} %get-tuple-element.41), channel_id=1, source_target_pairs={{0,248},{8,240},{16,232},{24,224},{32,216},{40,208},{48,200},{56,1... | collective-permute-start | bytes 258056 | tf_op jit(solution)/shard_map/ppermute | solution.py:634
  18.5 2.4 %collective-permute-start.3 = (f32[168,128]{1,0:T(8,128)S(1)}, f32[168,128]{1,0:T(8,128)S(1)}, u32[]{:S(2)}, u32[]{:S(2)}) collective-permute-start(f32[168,128]{1,0:T(8,128)S(1)} %get-tuple-element.42), channel_id=1, source_target_pairs={{0,1},{8,9},{16,17},{24,25},{32,33},{40,41},{48,49},{56,57},{64,65... | collective-permute-start | bytes 258056 | tf_op jit(solution)/shard_map/ppermute | solution.py:634
  20.9 6.7 %shard_map.96 = (f32[15,96,128]{2,1,0:T(8,128)}, f32[15,96,128]{2,1,0:T(8,128)}, f32[15,96,128]{2,1,0:T(8,128)}, f32[15,96,128]{2,1,0:T(8,128)}, f32[5,15,8,128]...) custom-call(s32[2]{0:T(128)S(1)} %pad_add_fusion.place._, ...), custom_call_target="tpu_custom_call" | custom-call | flops 50000000 | bytes 4000000 | tf_op jit(solution)/shard_map/pallas_call | solution.py:602
  27.6 0.0 collective-permute-done.2.got_x
  27.6 0.0 collective-permute-done.3.got_y
  27.6 3.0 %shard_map.97 = (f32[15,96,128]{2,1,0:T(8,128)}, f32[15,96,128]{2,1,0:T(8,128)}, f32[15,96,128]{2,1,0:T(8,128)}, f32[15,96,128]{2,1,0:T(8,128)}) custom-call(s32[2]{0:T(128)S(1)} %pad_add_fusion.place._, f32[2,168,128]{2,1,0:T(8,128)S(1)} %get-tuple-element.40.own, ...), custom_call_target="tpu_custom_call", output_to_operand_aliasing={{0}: (7, {}), {1}: (8, {}), {2}: (9, {}), {3}: (10, {})} | custom-call | flops 2000000 | bytes 4000000 | tf_op jit(solution)/shard_map/pallas_call | solution.py:602
Async XLA Ops:
  4.1 10.6 %collective-permute-start = (f32[160,128]{1,0:T(8,128)S(1)}, f32[160,128]{1,0:T(8,128)S(1)}, u32[]{:S(2)}, u32[]{:S(2)}) collective-permute-start(f32[160,128]{1,0:T(8,128)S(1)} %get-tuple-element.28), channel_id=1, source_target_pairs={{0,8},{8,0},{16,24},{24,16},{32,40},{40,32},{48,56},{56,48},{64,72... | collective-permute-start | bytes 245768 | tf_op jit(solution)/shard_map/ppermute | solution.py:634
  4.2 10.5 %collective-permute-start.1 = (f32[160,128]{1,0:T(8,128)S(1)}, f32[160,128]{1,0:T(8,128)S(1)}, u32[]{:S(2)}, u32[]{:S(2)}) collective-permute-start(f32[160,128]{1,0:T(8,128)S(1)} %get-tuple-element.29), channel_id=1, source_target_pairs={{0,248},{8,16},{16,8},{24,32},{32,24},{40,48},{48,40},{56,64},{64,... | collective-permute-start | bytes 245768 | tf_op jit(solution)/shard_map/ppermute | solution.py:634
  15.5 12.0 %collective-permute-start.2 = (f32[168,128]{1,0:T(8,128)S(1)}, f32[168,128]{1,0:T(8,128)S(1)}, u32[]{:S(2)}, u32[]{:S(2)}) collective-permute-start(f32[168,128]{1,0:T(8,128)S(1)} %get-tuple-element.41), channel_id=1, source_target_pairs={{0,248},{8,240},{16,232},{24,224},{32,216},{40,208},{48,200},{56,1... | collective-permute-start | bytes 258056 | tf_op jit(solution)/shard_map/ppermute | solution.py:634
  18.5 9.0 %collective-permute-start.3 = (f32[168,128]{1,0:T(8,128)S(1)}, f32[168,128]{1,0:T(8,128)S(1)}, u32[]{:S(2)}, u32[]{:S(2)}) collective-permute-start(f32[168,128]{1,0:T(8,128)S(1)} %get-tuple-element.42), channel_id=1, source_target_pairs={{0,1},{8,9},{16,17},{24,25},{32,33},{40,41},{48,49},{56,57},{64,65... | collective-permute-start | bytes 258056 | tf_op jit(solution)/shard_map/ppermute | solution.py:634

commit v4 on v3

--- a/solution.py
+++ b/solution.py
@@ -195,10 +195,13 @@
     sub = iota((TILE, COLS), 0)
     group = jnp.where(lane % 8 < 4, lane // 8, -1)
     inside = pl.ds(PAD, ROWS)
-    copies = [pltpu.make_async_copy(x, field[f].at[:, inside, :], sems.at[f]) for f, x in enumerate((t, s, u, v))]
+    half = ROWS // 2
+    copies = [pltpu.make_async_copy(x, field[f].at[:, inside, :], sems.at[f]) for f, x in enumerate((t, s, u))]
+    copies.append(pltpu.make_async_copy(v.at[:, 0:half, :], v_in.at[:, PAD:PAD + half, :], sems.at[3]))
     copies.append(pltpu.make_async_copy(flag, held_flag, sems.at[4]))
     copies.append(pltpu.make_async_copy(tally, held_tally, sems.at[5]))
-    for f in (4, 5, 0, 1, 2, 3):
+    copies.append(pltpu.make_async_copy(v.at[:, half:ROWS, :], v_in.at[:, PAD + half:PAD + ROWS, :], sems.at[6]))
+    for f in (4, 5, 0, 1, 2, 3, 6):
         copies[f].start()
     copies[4].wait()
     copies[5].wait()
@@ -234,6 +237,8 @@
         if f < STATE:
             copies[f].wait()
         for b in range(BLOCKS):
+            if f == 3 and b == BLOCKS // 2:
+                copies[6].wait()
             gather(f, b)
             if f != 3 and b % 4 == 3:
                 couple(3 * (0 if f == 4 else f + 1) + b // 4)
@@ -638,7 +643,7 @@
     message = (MESSAGE, COLS)
     col_p, col_q, own_cols, rows, wet, *padded, open_e, link, spin = call(
         pack_kernel, place, (t, s, u, v, flag, tally), [(PACK, COLS), (PACK, COLS), square, (2, EDGE_AT, COLS)] + [tall] * 5
-        + [deep, (3,) + deep, (ROWS, COLS)], [pltpu.VMEM(deep, jnp.int32), pltpu.VMEM((ROWS, COLS), jnp.int32), pltpu.SemaphoreType.DMA((6,)), square],
+        + [deep, (3,) + deep, (ROWS, COLS)], [pltpu.VMEM(deep, jnp.int32), pltpu.VMEM((ROWS, COLS), jnp.int32), pltpu.SemaphoreType.DMA((7,)), square],
         12, 1_000_000, far_in=6)
     got_p, got_q = send(col_p, pairs_p), send(col_q, pairs_q)
     field1, = call(lambda _, *refs: first_kernel(*refs), place, (*padded, wet, open_e, link, spin), [(STATE,) + tall],

time: 30.8 us -> 30.9 us (level)
  no operation moved by 1% of the time
where the time goes in v4:
time: 30.9 us; the launch traced here: 30.8 us
  Pallas kernels  17.6 us (57%)
  starting transfers between devices  12.3 us (40%)
  between operations  0.86 us (3%)
    pallas_call x5, Pallas kernels, call(): pl.pallas_call(kernel, out_shape=[jax.ShapeDtypeStruct(o, F32) if i < far...  17.6 us
    ppermute x4, starting transfers between devices, send(): return lax.ppermute(x, ('lon', 'lat'), pairs)  12.3 us
  transfers between devices with their start and end apart: 4, of which 0 were waited for; matrix products, arithmetic and copies ran while one was open for 0% of the time, Pallas kernels for 33%

profile of v4, /device:TPU:24, one launch (start us, length us, event | category | flops | bytes accessed | tf_op | source)
XLA Modules:
  0.0 30.8 jit_solution(10075104627648399296)
XLA Ops:
  0.6 0.1 pad_add_fusion.place._
  0.7 3.5 %shard_map.93 = (f32[160,128]{1,0:T(8,128)S(1)}, f32[160,128]{1,0:T(8,128)S(1)}, f32[5,128,128]{2,1,0:T(8,128)S(1)}, f32[2,152,128]{2,1,0:T(8,128)S(1)}, f32[15,...) custom-call(s32[2]{0:T(128)S(1)} %pad_add_fusion.place._, ...), custom_call_target="tpu_custom_call" | custom-call | flops 1000000 | bytes 4000000 | tf_op jit(solution)/shard_map/pallas_call | solution.py:607
  4.2 0.1 collective-permute-start
  4.3 6.9 %collective-permute-start.1 = (f32[160,128]{1,0:T(8,128)S(1)}, f32[160,128]{1,0:T(8,128)S(1)}, u32[]{:S(2)}, u32[]{:S(2)}) collective-permute-start(f32[160,128]{1,0:T(8,128)S(1)} %get-tuple-element.29), channel_id=1, source_target_pairs={{0,248},{8,16},{16,8},{24,32},{32,24},{40,48},{48,40},{56,64},{64,... | collective-permute-start | bytes 245768 | tf_op jit(solution)/shard_map/ppermute | solution.py:639
  11.2 3.6 %shard_map.94._.field1 = f32[4,15,112,128]{3,2,1,0:T(8,128)S(1)} custom-call(s32[2]{0:T(128)S(1)} %pad_add_fusion.place._, f32[15,112,128]{2,1,0:T(8,128)S(1)} %get-tuple-element.32.refs_0_, f32[15,112,128]{2,1,0:T(8,128)S(1)} %get-tuple-element.33.refs_1_, f32[15,112,128]{2,1,0:T(8,128)S(1)} %get-tuple-element.34.refs_2_, ...), custom_call_target="tpu_custom_call" | custom-call | flops 40000000 | bytes 4000000 | tf_op jit(solution)/shard_map/pallas_call | solution.py:607
  14.8 0.0 collective-permute-done.got_p
  14.8 0.0 collective-permute-done.1.got_q
  14.9 0.8 %shard_map.95 = (f32[5,128,128]{2,1,0:T(8,128)S(1)}, f32[5,128,128]{2,1,0:T(8,128)S(1)}, f32[2,168,128]{2,1,0:T(8,128)S(1)}, f32[168,128]{1,0:T(8,128)S(1)}, f32[168,128]{1,0:T(8,128)S(1)}) custom-call(s32[2]{0:T(128)S(1)} %pad_add_fusion.place._, f32[160,128]{1,0:T(8,128)S(1)} %collective-permute-done.got_p, f32[160,128]{1,0:T(8,128)S(1)} %collective-permute-done.1.got_q, ...), custom_call_target="tpu_custom_call" | custom-call | flops 1000000 | bytes 4000000 | tf_op jit(solution)/shard_map/pallas_call | solution.py:607
  15.6 3.0 %collective-permute-start.2 = (f32[168,128]{1,0:T(8,128)S(1)}, f32[168,128]{1,0:T(8,128)S(1)}, u32[]{:S(2)}, u32[]{:S(2)}) collective-permute-start(f32[168,128]{1,0:T(8,128)S(1)} %get-tuple-element.41), channel_id=1, source_target_pairs={{0,248},{8,240},{16,232},{24,224},{32,216},{40,208},{48,200},{56,1... | collective-permute-start | bytes 258056 | tf_op jit(solution)/shard_map/ppermute | solution.py:639
  18.6 2.4 %collective-permute-start.3 = (f32[168,128]{1,0:T(8,128)S(1)}, f32[168,128]{1,0:T(8,128)S(1)}, u32[]{:S(2)}, u32[]{:S(2)}) collective-permute-start(f32[168,128]{1,0:T(8,128)S(1)} %get-tuple-element.42), channel_id=1, source_target_pairs={{0,1},{8,9},{16,17},{24,25},{32,33},{40,41},{48,49},{56,57},{64,65... | collective-permute-start | bytes 258056 | tf_op jit(solution)/shard_map/ppermute | solution.py:639
  21.0 6.7 %shard_map.96 = (f32[15,96,128]{2,1,0:T(8,128)}, f32[15,96,128]{2,1,0:T(8,128)}, f32[15,96,128]{2,1,0:T(8,128)}, f32[15,96,128]{2,1,0:T(8,128)}, f32[5,15,8,128]...) custom-call(s32[2]{0:T(128)S(1)} %pad_add_fusion.place._, ...), custom_call_target="tpu_custom_call" | custom-call | flops 50000000 | bytes 4000000 | tf_op jit(solution)/shard_map/pallas_call | solution.py:607
  27.7 0.0 collective-permute-done.2.got_x
  27.7 0.0 collective-permute-done.3.got_y
  27.7 3.0 %shard_map.97 = (f32[15,96,128]{2,1,0:T(8,128)}, f32[15,96,128]{2,1,0:T(8,128)}, f32[15,96,128]{2,1,0:T(8,128)}, f32[15,96,128]{2,1,0:T(8,128)}) custom-call(s32[2]{0:T(128)S(1)} %pad_add_fusion.place._, f32[2,168,128]{2,1,0:T(8,128)S(1)} %get-tuple-element.40.own, ...), custom_call_target="tpu_custom_call", output_to_operand_aliasing={{0}: (7, {}), {1}: (8, {}), {2}: (9, {}), {3}: (10, {})} | custom-call | flops 2000000 | bytes 4000000 | tf_op jit(solution)/shard_map/pallas_call | solution.py:607
Async XLA Ops:
  4.2 10.6 %collective-permute-start = (f32[160,128]{1,0:T(8,128)S(1)}, f32[160,128]{1,0:T(8,128)S(1)}, u32[]{:S(2)}, u32[]{:S(2)}) collective-permute-start(f32[160,128]{1,0:T(8,128)S(1)} %get-tuple-element.28), channel_id=1, source_target_pairs={{0,8},{8,0},{16,24},{24,16},{32,40},{40,32},{48,56},{56,48},{64,72... | collective-permute-start | bytes 245768 | tf_op jit(solution)/shard_map/ppermute | solution.py:639
  4.3 10.5 %collective-permute-start.1 = (f32[160,128]{1,0:T(8,128)S(1)}, f32[160,128]{1,0:T(8,128)S(1)}, u32[]{:S(2)}, u32[]{:S(2)}) collective-permute-start(f32[160,128]{1,0:T(8,128)S(1)} %get-tuple-element.29), channel_id=1, source_target_pairs={{0,248},{8,16},{16,8},{24,32},{32,24},{40,48},{48,40},{56,64},{64,... | collective-permute-start | bytes 245768 | tf_op jit(solution)/shard_map/ppermute | solution.py:639
  15.6 12.0 %collective-permute-start.2 = (f32[168,128]{1,0:T(8,128)S(1)}, f32[168,128]{1,0:T(8,128)S(1)}, u32[]{:S(2)}, u32[]{:S(2)}) collective-permute-start(f32[168,128]{1,0:T(8,128)S(1)} %get-tuple-element.41), channel_id=1, source_target_pairs={{0,248},{8,240},{16,232},{24,224},{32,216},{40,208},{48,200},{56,1... | collective-permute-start | bytes 258056 | tf_op jit(solution)/shard_map/ppermute | solution.py:639
  18.6 9.0 %collective-permute-start.3 = (f32[168,128]{1,0:T(8,128)S(1)}, f32[168,128]{1,0:T(8,128)S(1)}, u32[]{:S(2)}, u32[]{:S(2)}) collective-permute-start(f32[168,128]{1,0:T(8,128)S(1)} %get-tuple-element.42), channel_id=1, source_target_pairs={{0,1},{8,9},{16,17},{24,25},{32,33},{40,41},{48,49},{56,57},{64,65... | collective-permute-start | bytes 258056 | tf_op jit(solution)/shard_map/ppermute | solution.py:639
